TPU v7x, 32 devices: a whole 2x2x4 slice. The times are simulated.
32 devices in a mesh: seq: 8 (over z, x), exp: 4 (over y, core).
Axes of the slice: x: 2, y: 2, z: 4, core: 2. Of those that a mesh axis runs over, the one named last changes fastest.
Arguments:
- stream: bfloat16 [4096, 2048], P(('seq', 'exp')), may hold values from -6 to 6
- moe_gain: float32 [2048], replicated, may hold values from 0.1 to 1.9
- expert_ids: int32 [4096, 10], P(('seq', 'exp')), may hold values from 0 to 63, all different within a row; in each aligned block of 128 rows (0 to 127, 128 to 255, ...) at most 24 rows name the same one
- expert_weights: float32 [4096, 10], P(('seq', 'exp')), may hold values from 0.02 to 0.3
- gate_up_weight: bfloat16 [64, 2048, 1024], P(('seq', 'exp')), may hold values from -0.125 to 0.125
- down: bfloat16 [64, 512, 2048], P(('seq', 'exp')), may hold values from -0.25 to 0.25
- mixer_gain: float32 [2048], replicated, may hold values from 0.1 to 1.9
- qkv_weight: bfloat16 [3, 2048, 4096], P(None, None, 'exp'), may hold values from -0.125 to 0.125
- decay_log: float32 [4096, 32], P('seq', 'exp'), may hold values from -2 to 0
- write_rate: float32 [4096, 32], P('seq', 'exp'), may hold values from 0 to 1
Outputs:
- mixed: bfloat16 [4096, 2048], P(('seq', 'exp'))
- core: float32 [4096, 4096], P('seq', 'exp')
Inputs may be any that keep to these rules, and one draw needn't show every extreme that they name: `expert_ids`: each token names 10 different experts. Among the 128 tokens of one device at most 24 name the same expert, and in every draw some expert is named by exactly 24 tokens of some device.
All inputs are finite; a program needn't handle non-finite values.
Results may differ from a plain program's by a relative error of at most 0.0081.
Values may be sent and summed in bfloat16 or wider, within the bound.
No kernel may reach another device: no remote copies, remote signals or barrier semaphores. Data moves between devices by JAX's collectives and lax.ppermute only.
A program may use at most 128 MiB of HBM per device.

v0:
```python
from functools import partial

import jax
import jax.numpy as jnp
from jax import lax
from jax.sharding import PartitionSpec as P

CH = 128


def from_behind(x, axis, by):
    count = lax.axis_size(axis)
    pairs = [(i, i + by) for i in range(count) if 0 <= i + by < count]
    return lax.ppermute(x, axis, pairs)


def rms_scale(values, gain):
    wide = values.astype(jnp.float32)
    return wide * lax.rsqrt(jnp.mean(wide * wide, axis=-1, keepdims=True) + 1e-06) * gain


def unit_rows(values):
    return values * lax.rsqrt(jnp.sum(values * values, axis=-1, keepdims=True) + 1e-06)


def local(
    stream,
    moe_gain,
    expert_ids,
    expert_weights,
    gate_up_weight,
    down,
    mixer_gain,
    qkv_weight,
    decay_log,
    write_rate,
):
    tok_rows, width = stream.shape
    choose = expert_ids.shape[1]
    local_experts = gate_up_weight.shape[0]
    expert_width = down.shape[1]
    seq_count = lax.axis_size("seq")
    exp_count = lax.axis_size("exp")
    devices = seq_count * exp_count
    experts_all = local_experts * devices
    capacity = max(2, (tok_rows * choose * 6 + experts_all * 5 - 1) // (experts_all * 5))
    normed = rms_scale(stream, moe_gain).astype(jnp.bfloat16)
    flat_ids = expert_ids.reshape(-1)
    onehot = (flat_ids[:, None] == jnp.arange(experts_all, dtype=jnp.int32)[None, :]).astype(
        jnp.int32
    )
    rank = jnp.sum(jnp.cumsum(onehot, axis=0) * onehot, axis=1) - 1
    slot = flat_ids * capacity + rank
    token_of = jnp.arange(tok_rows * choose, dtype=jnp.int32) // choose
    send = jnp.zeros((experts_all * capacity, width), jnp.bfloat16).at[slot].set(normed[token_of])
    outbound = send.reshape(devices, local_experts, capacity, width)
    both = jnp.einsum(
        "secd,edf->secf",
        lax.all_to_all(outbound, ("seq", "exp"), split_axis=0, concat_axis=0, tiled=True),
        gate_up_weight,
        preferred_element_type=jnp.float32,
    )
    hidden = (jax.nn.silu(both[..., :expert_width]) * both[..., expert_width:]).astype(jnp.bfloat16)
    gathered_rows = lax.all_to_all(
        jnp.einsum("secf,efd->secd", hidden, down, preferred_element_type=jnp.float32).astype(
            jnp.bfloat16
        ),
        ("seq", "exp"),
        split_axis=0,
        concat_axis=0,
        tiled=True,
    )
    back_rows = gathered_rows.reshape(experts_all * capacity, width)[slot].astype(jnp.float32)
    moe = jnp.sum(back_rows.reshape(tok_rows, choose, width) * expert_weights[:, :, None], axis=1)
    mixed = (stream.astype(jnp.float32) + moe).astype(jnp.bfloat16)
    normed_mix = rms_scale(mixed, mixer_gain).astype(jnp.bfloat16)
    projected = jnp.einsum(
        "rd,pde->pre",
        lax.all_gather(normed_mix, "exp", axis=0, tiled=True),
        qkv_weight,
        preferred_element_type=jnp.float32,
    )
    length = projected.shape[1]
    heads = decay_log.shape[1]
    head_dim = projected.shape[2] // heads
    blocks = length // CH
    highest = lax.Precision.HIGHEST
    product = partial(jnp.einsum, precision=highest)

    def to_blocks(values):
        return values.reshape(blocks, CH, heads, head_dim).transpose(2, 0, 1, 3)

    query = to_blocks(unit_rows(projected[0].reshape(length, heads, head_dim)))
    key = to_blocks(unit_rows(projected[1].reshape(length, heads, head_dim)))
    value = to_blocks(projected[2].reshape(length, heads, head_dim))
    decay = decay_log.reshape(blocks, CH, heads).transpose(2, 0, 1)
    delta_step_size = write_rate.reshape(blocks, CH, heads).transpose(2, 0, 1)
    cumulative = jnp.cumsum(decay, axis=-1)
    spread = cumulative[..., :, None] - cumulative[..., None, :]
    element_offsets = jnp.arange(CH, dtype=jnp.int32)
    strict = element_offsets[:, None] > element_offsets[None, :]
    inclusive = element_offsets[:, None] >= element_offsets[None, :]
    key_key = product("hncd,hnjd->hncj", key, key)
    lower = jnp.where(
        strict,
        delta_step_size[..., :, None] * jnp.exp(jnp.where(strict, spread, 0.0)) * key_key,
        0.0,
    )
    identity_block = jnp.eye(CH, dtype=jnp.float32)
    inverse = identity_block - lower
    power = lower
    reach = 2
    while reach < CH:
        power = product("hnij,hnjk->hnik", power, power)
        inverse = inverse + product("hnij,hnjk->hnik", inverse, power)
        reach = reach * 2
    growth = jnp.exp(cumulative)
    weighted_keys = product("hncj,hnjd->hncd", inverse, (delta_step_size * growth)[..., None] * key)
    weighted_values = product("hncj,hnjd->hncd", inverse, delta_step_size[..., None] * value)
    last = cumulative[..., -1]
    key_end = jnp.exp(last[..., None] - cumulative)[..., None] * key
    identity_state = jnp.eye(head_dim, dtype=jnp.float32)
    transition = jnp.exp(last)[..., None, None] * identity_state - product(
        "hncd,hnce->hnde", key_end, weighted_keys
    )
    written = product("hncd,hnce->hnde", key_end, weighted_values)
    probe_lookup_product = product("hncd,hnjd->hncj", query, key)
    masked = jnp.where(
        inclusive, jnp.exp(jnp.where(inclusive, spread, 0.0)) * probe_lookup_product, 0.0
    )
    entering = growth[..., None] * query - product("hncj,hnjd->hncd", masked, weighted_keys)
    local_out = product("hncj,hnjd->hncd", masked, weighted_values)

    def compose(earlier, later):
        return (
            product("...ij,...jk->...ik", later[0], earlier[0]),
            product("...ij,...jk->...ik", later[0], earlier[1]) + later[1],
        )

    running_trans, running_written = lax.associative_scan(compose, (transition, written), axis=1)
    start_trans = jnp.concatenate(
        [jnp.broadcast_to(identity_state, (heads, 1, head_dim, head_dim)), running_trans[:, :-1]],
        axis=1,
    )
    start_written = jnp.concatenate(
        [jnp.zeros((heads, 1, head_dim, head_dim), jnp.float32), running_written[:, :-1]], axis=1
    )
    segment_trans = running_trans[:, -1]
    segment_written = running_written[:, -1]
    empty_state = jnp.zeros((heads, head_dim, head_dim), jnp.float32)

    def relay_step(step, incoming):
        outgoing = product("hij,hjk->hik", segment_trans, incoming) + segment_written
        return from_behind(outgoing, "seq", 1)

    arriving = lax.fori_loop(0, seq_count - 1, relay_step, empty_state)
    block_state = product("hnij,hjk->hnik", start_trans, arriving) + start_written
    outputs = local_out + product("hncd,hnde->hnce", entering, block_state)
    core = outputs.transpose(1, 2, 0, 3).reshape(length, heads * head_dim)
    return (mixed, core)


def solution(mesh):
    in_specs = (
        P(("seq", "exp"), None),
        P(),
        P(("seq", "exp"), None),
        P(("seq", "exp"), None),
        P(("seq", "exp"), None, None),
        P(("seq", "exp"), None, None),
        P(),
        P(None, None, "exp"),
        P("seq", "exp"),
        P("seq", "exp"),
    )
    out_specs = (P(("seq", "exp"), None), P("seq", "exp"))
    return jax.shard_map(local, mesh=mesh, in_specs=in_specs, out_specs=out_specs, check_vma=False)
```

profile of v0, /device:TPU:0, one launch (start us, length us, event | category | flops | bytes accessed | tf_op | source)
XLA Modules:
  0.0 709.7 jit_solution(7569415825621288429)
XLA Ops:
  9.0 18.1 %reduce-window.6 = s32[64,10,128]{2,1,0:T(8,128)S(1)} reduce-window(s32[64,10,128]{2,1,0:T(8,128)S(1)} %fusion.107, s32[]{:T(128)} %copy.116), window={size=1x1x128 pad=0_0x0_0x127_0}, to_apply=%region_0.0 | reduce-window | flops 10403840 | bytes 655364 | tf_op jit(solution)/shard_map/reduce-window
  28.9 34.1 %scatter_custom_fusion = bf16[1536,2048]{1,0:T(8,128)(2,1)} fusion(s32[1280]{0:T(1024)S(1)} %fusion.111, bf16[128,2048]{1,0:T(8,128)(2,1)S(1)} %fusion.70, s32[2048]{0:T(1024)S(1)} %pad_clamp_fusion.1, bf16[]{:T(256)} %constant.16.clone.1), kind=kCustom, calls=%fused_computation.9 | custom fusion | bytes 6291458 | tf_op jit(solution)/shard_map/scatter | solution.py:55
  62.9 145.9 %all_to_all.10 = bf16[32,2,24,2048]{3,2,1,0:T(8,128)(2,1)S(1)} all-to-all(bf16[32,2,24,2048]{3,2,1,0:T(8,128)(2,1)} %bitcast.178), channel_id=1, replica_groups=mesh['seq'=8,'exp'=4] {'seq','exp'}, dimensions={0} | all-to-all | bytes 12582912 | tf_op jit(solution)/shard_map/all_to_all | solution.py:59
  208.8 10.9 %fusion.8 = f32[32,2,24,1024]{3,2,0,1:T(8,128)} fusion(bf16[2,2048,1024]{2,1,0:T(8,128)(2,1)} %param.16, bf16[32,2,24,2048]{3,2,1,0:T(8,128)(2,1)S(1)} %all_to_all.10), kind=kOutput, calls=%fused_computation.17 | convolution fusion | flops 6442450944 | bytes 20971520 | tf_op jit(solution)/shard_map/secd,edf->secf/dot_general | solution.py:57
  219.8 6.8 convert_bitcast_fusion
  234.3 139.4 %all-to-all-done.1 = bf16[32,2,24,2048]{3,2,1,0:T(8,128)(2,1)} async-done(((bf16[32,2,24,2048]{3,2,1,0:T(8,128)(2,1)}), bf16[32,2,24,2048]{3,2,1,0:T(8,128)(2,1)}, u32[]{:S(2)}, u32[]{:S(2)}) %all-to-all-start.1) | async-done | bytes 6291488 | tf_op jit(solution)/shard_map/all_to_all | solution.py:64
  373.8 14.4 %gather_fusion = bf16[1280,2048]{1,0:T(8,128)(2,1)} fusion(bf16[1536,2048]{1,0:T(8,128)(2,1)} %bitcast.9, s32[2048]{0:T(1024)S(1)} %pad_clamp_fusion), kind=kCustom, calls=%fused_computation.1 | custom fusion | bytes 10490880 | tf_op jit(solution)/shard_map/gather | solution.py:73
  388.2 10.4 %reshape.226 = f32[128,10,2048]{2,1,0:T(8,128)} reshape(bf16[1280,2048]{1,0:T(8,128)(2,1)} %gather_fusion) | data formatting | bytes 15728640 | tf_op jit(solution)/shard_map/convert_element_type | solution.py:73
  398.5 9.5 %multiply_reduce_fusion = f32[128,2048]{1,0:T(8,128)S(1)} fusion(f32[128,10,2048]{2,1,0:T(8,128)} %reshape.226, f32[128,10]{1,0:T(8,128)S(1)} %copy.57), kind=kLoop, calls=%fused_computation.4 | loop fusion | flops 4980736 | bytes 11539456 | tf_op jit(solution)/shard_map/reduce_sum | solution.py:74
  411.8 22.1 %all-gather.2.cloned.1.call-done = bf16[512,2048]{1,0:T(8,128)(2,1)} async-done(((bf16[128,2048]{1,0:T(8,128)(2,1)}), bf16[512,2048]{1,0:T(8,128)(2,1)}) %all-gather.2.cloned.1.call-update) | async-done | bytes 2097168 | tf_op jit(solution)/shard_map/all_gather | solution.py:79
  433.9 9.9 %convolution_bitcast_fusion = f32[3,512,1024]{2,1,0:T(8,128)S(1)} fusion(bf16[3,2048,1024]{2,1,0:T(8,128)(2,1)} %param.19, bf16[512,2048]{1,0:T(8,128)(2,1)} %all-gather.2.cloned.1.call-done), kind=kOutput, calls=%fused_computation.18 | convolution fusion | flops 6442450944 | bytes 20971520 | tf_op jit(solution)/shard_map/rd,pde->pre/dot_general | solution.py:77
  457.4 4.5 fusion.19
  490.4 4.5 fusion.29
  509.9 10.0 %pad.47 = f32[8,3,128,128]{3,2,1,0:T(8,128)} pad(f32[8,2,128,128]{3,2,1,0:T(8,128)} %pad_maximum_fusion.1, f32[]{:T(128)} %constant.26.clone.1), padding=0_0_0x0_0_1x0_0_0x0_0_0 | pad | bytes 2621444 | tf_op jit(solution)/shard_map/slice | solution.py:146
  519.9 10.4 %pad.33 = f32[8,4,128,128]{3,2,1,0:T(8,128)} pad(f32[8,2,128,128]{3,2,1,0:T(8,128)} %pad_maximum_fusion.1, f32[]{:T(128)} %constant.26.clone.1), padding=0_0_0x0_1_1x0_0_0x0_0_0 | pad | bytes 3145732 | tf_op jit(solution)/shard_map/pad | solution.py:140
  533.3 6.3 pad.88
  539.6 6.4 pad.30
  565.8 7.1 pad.34
  574.0 10.4 %pad.29 = f32[8,4,128,128]{3,2,1,0:T(8,128)} pad(f32[8,2,128,128]{3,2,1,0:T(8,128)} %pad_maximum_fusion, f32[]{:T(128)} %constant.26.clone.1), padding=0_0_0x0_1_1x0_0_0x0_0_0 | pad | bytes 3145732 | tf_op jit(solution)/shard_map/pad | solution.py:140
  590.8 100.6 %while.10 = (s32[]{:T(128)}, f32[8,128,128]{2,1,0:T(8,128)S(1)}, f32[8,128,128]{2,1,0:T(8,128)S(1)}, f32[8,128,128]{2,1,0:T(8,128)S(1)}, s32[]{:T(128)}) while((s32[]{:T(128)}, f32[8,128,128]{2,1,0:T(8,128)S(1)}, f32[8,128,128]{2,1,0:T(8,128)S(1)}, f32[8,128,128]{2,1,0:T(8,128)S(1)}, s32[]{:T(128)}) %tuple.30), condition=%wide.region_11.12_spmd, body=%wide.region_10.11_spmd.sunk | while | flops 201457664 | bytes 4194405 | solution.py:156
  594.9 11.5 %collective-permute-done = f32[8,128,128]{2,1,0:T(8,128)S(1)} collective-permute-done((f32[8,128,128]{2,1,0:T(8,128)S(1)}, f32[8,128,128]{2,1,0:T(8,128)S(1)}, u32[]{:S(2)}, u32[]{:S(2)}) %collective-permute-start) | collective-permute-done | bytes 524320 | tf_op jit(solution)/shard_map/while/body/eval_jaxpr/ppermute | solution.py:14
  611.5 10.7 %collective-permute-done = f32[8,128,128]{2,1,0:T(8,128)S(1)} collective-permute-done((f32[8,128,128]{2,1,0:T(8,128)S(1)}, f32[8,128,128]{2,1,0:T(8,128)S(1)}, u32[]{:S(2)}, u32[]{:S(2)}) %collective-permute-start) | collective-permute-done | bytes 524320 | tf_op jit(solution)/shard_map/while/body/eval_jaxpr/ppermute | solution.py:14
  627.3 9.8 %collective-permute-done = f32[8,128,128]{2,1,0:T(8,128)S(1)} collective-permute-done((f32[8,128,128]{2,1,0:T(8,128)S(1)}, f32[8,128,128]{2,1,0:T(8,128)S(1)}, u32[]{:S(2)}, u32[]{:S(2)}) %collective-permute-start) | collective-permute-done | bytes 524320 | tf_op jit(solution)/shard_map/while/body/eval_jaxpr/ppermute | solution.py:14
  637.7 5.2 collective-permute-start
  642.9 8.9 %collective-permute-done = f32[8,128,128]{2,1,0:T(8,128)S(1)} collective-permute-done((f32[8,128,128]{2,1,0:T(8,128)S(1)}, f32[8,128,128]{2,1,0:T(8,128)S(1)}, u32[]{:S(2)}, u32[]{:S(2)}) %collective-permute-start) | collective-permute-done | bytes 524320 | tf_op jit(solution)/shard_map/while/body/eval_jaxpr/ppermute | solution.py:14
  652.4 5.3 collective-permute-start
  657.8 7.9 %collective-permute-done = f32[8,128,128]{2,1,0:T(8,128)S(1)} collective-permute-done((f32[8,128,128]{2,1,0:T(8,128)S(1)}, f32[8,128,128]{2,1,0:T(8,128)S(1)}, u32[]{:S(2)}, u32[]{:S(2)}) %collective-permute-start) | collective-permute-done | bytes 524320 | tf_op jit(solution)/shard_map/while/body/eval_jaxpr/ppermute | solution.py:14
  666.4 5.3 collective-permute-start
  671.7 7.0 collective-permute-done
  679.4 5.3 collective-permute-start
  684.7 6.6 collective-permute-done
  694.9 4.6 add_bitcast_fusion
  (153 shorter events, 125.0 us)
Async XLA Ops:
  9.0 19.4 %copy-start.14 = (bf16[128,2048]{1,0:T(8,128)(2,1)S(1)}, bf16[128,2048]{1,0:T(8,128)(2,1)}, u32[]{:S(2)}) copy-start(bf16[128,2048]{1,0:T(8,128)(2,1)} %param.12) | copy-start | bytes 1572868
  27.2 1.5 copy-start.19
  208.8 10.9 %copy-start.22 = (bf16[2,512,2048]{2,1,0:T(8,128)(2,1)S(1)}, bf16[2,512,2048]{2,1,0:T(8,128)(2,1)}, u32[]{:S(2)}) copy-start(bf16[2,512,2048]{2,1,0:T(8,128)(2,1)} %param.17) | copy-start | bytes 12582916
  229.9 4.3 copy-start.21
  229.9 143.9 %all-to-all-start.1 = ((bf16[32,2,24,2048]{3,2,1,0:T(8,128)(2,1)}), bf16[32,2,24,2048]{3,2,1,0:T(8,128)(2,1)}, u32[]{:S(2)}, u32[]{:S(2)}) async-start(bf16[32,2,24,2048]{3,2,1,0:T(8,128)(2,1)} %copy.56), calls=%async_computation.1 | async-start | bytes 12582912 | tf_op jit(solution)/shard_map/all_to_all | solution.py:64
  233.7 200.2 %all-gather.2.cloned.1.call-start = ((), (), s32[]{:S(2)}) async-start(), calls=%async_computation.2 | async-start | bytes 2621440 | tf_op jit(solution)/shard_map/all_gather | solution.py:79
  408.1 2.1 copy-start.18
  408.1 3.2 copy-start.17
  485.2 2.2 copy-start.11
  494.9 6.3 copy-start.4
  497.4 1.4 copy-start.2
  501.2 5.7 copy-start.8
  503.8 3.1 copy-start
  507.6 1.2 slice-start.1
  530.3 1.6 copy-start.1
  553.9 1.3 copy-start.6
  555.2 2.5 copy-start.5
  557.7 4.0 copy-start.3
  565.8 7.1 slice-start
  565.8 7.1 copy-start.16
  572.8 11.6 %copy-start.10 = (f32[8,4,128,128]{3,2,1,0:T(8,128)}, f32[8,4,128,128]{3,2,1,0:T(8,128)S(1)}, u32[]{:S(2)}) copy-start(f32[8,4,128,128]{3,2,1,0:T(8,128)S(1)} %pad.34) | copy-start | bytes 6291460
  584.4 4.5 copy-start.13
  587.3 2.1 copy-start.12
  591.4 14.9 %collective-permute-start = (f32[8,128,128]{2,1,0:T(8,128)S(1)}, f32[8,128,128]{2,1,0:T(8,128)S(1)}, u32[]{:S(2)}, u32[]{:S(2)}) collective-permute-start(f32[8,128,128]{2,1,0:T(8,128)S(1)} %convolution_add_fusion.6), channel_id=1, source_target_pairs={{0,4},{4,8},{8,12},{12,16},{16,20},{20,24},{24,28},{1,5},{5,9},{9,... | collective-permute-start | bytes 1572872 | tf_op jit(solution)/shard_map/while/body/eval_jaxpr/ppermute | solution.py:14
  607.0 15.1 %collective-permute-start = (f32[8,128,128]{2,1,0:T(8,128)S(1)}, f32[8,128,128]{2,1,0:T(8,128)S(1)}, u32[]{:S(2)}, u32[]{:S(2)}) collective-permute-start(f32[8,128,128]{2,1,0:T(8,128)S(1)} %convolution_add_fusion.6), channel_id=1, source_target_pairs={{0,4},{4,8},{8,12},{12,16},{16,20},{20,24},{24,28},{1,5},{5,9},{9,... | collective-permute-start | bytes 1572872 | tf_op jit(solution)/shard_map/while/body/eval_jaxpr/ppermute | solution.py:14
  622.8 14.2 %collective-permute-start = (f32[8,128,128]{2,1,0:T(8,128)S(1)}, f32[8,128,128]{2,1,0:T(8,128)S(1)}, u32[]{:S(2)}, u32[]{:S(2)}) collective-permute-start(f32[8,128,128]{2,1,0:T(8,128)S(1)} %convolution_add_fusion.6), channel_id=1, source_target_pairs={{0,4},{4,8},{8,12},{12,16},{16,20},{20,24},{24,28},{1,5},{5,9},{9,... | collective-permute-start | bytes 1572872 | tf_op jit(solution)/shard_map/while/body/eval_jaxpr/ppermute | solution.py:14
  637.7 14.1 %collective-permute-start = (f32[8,128,128]{2,1,0:T(8,128)S(1)}, f32[8,128,128]{2,1,0:T(8,128)S(1)}, u32[]{:S(2)}, u32[]{:S(2)}) collective-permute-start(f32[8,128,128]{2,1,0:T(8,128)S(1)} %convolution_add_fusion.6), channel_id=1, source_target_pairs={{0,4},{4,8},{8,12},{12,16},{16,20},{20,24},{24,28},{1,5},{5,9},{9,... | collective-permute-start | bytes 1572872 | tf_op jit(solution)/shard_map/while/body/eval_jaxpr/ppermute | solution.py:14
  652.4 13.3 %collective-permute-start = (f32[8,128,128]{2,1,0:T(8,128)S(1)}, f32[8,128,128]{2,1,0:T(8,128)S(1)}, u32[]{:S(2)}, u32[]{:S(2)}) collective-permute-start(f32[8,128,128]{2,1,0:T(8,128)S(1)} %convolution_add_fusion.6), channel_id=1, source_target_pairs={{0,4},{4,8},{8,12},{12,16},{16,20},{20,24},{24,28},{1,5},{5,9},{9,... | collective-permute-start | bytes 1572872 | tf_op jit(solution)/shard_map/while/body/eval_jaxpr/ppermute | solution.py:14
  666.4 12.3 %collective-permute-start = (f32[8,128,128]{2,1,0:T(8,128)S(1)}, f32[8,128,128]{2,1,0:T(8,128)S(1)}, u32[]{:S(2)}, u32[]{:S(2)}) collective-permute-start(f32[8,128,128]{2,1,0:T(8,128)S(1)} %convolution_add_fusion.6), channel_id=1, source_target_pairs={{0,4},{4,8},{8,12},{12,16},{16,20},{20,24},{24,28},{1,5},{5,9},{9,... | collective-permute-start | bytes 1572872 | tf_op jit(solution)/shard_map/while/body/eval_jaxpr/ppermute | solution.py:14
  679.4 12.0 %collective-permute-start = (f32[8,128,128]{2,1,0:T(8,128)S(1)}, f32[8,128,128]{2,1,0:T(8,128)S(1)}, u32[]{:S(2)}, u32[]{:S(2)}) collective-permute-start(f32[8,128,128]{2,1,0:T(8,128)S(1)} %convolution_add_fusion.6), channel_id=1, source_target_pairs={{0,4},{4,8},{8,12},{12,16},{16,20},{20,24},{24,28},{1,5},{5,9},{9,... | collective-permute-start | bytes 1572872 | tf_op jit(solution)/shard_map/while/body/eval_jaxpr/ppermute | solution.py:14
  691.4 3.5 copy-start.7
  691.4 3.5 copy-start.9
  (2 other events, 1.9 us)
Sparse Core Ops, SparseCore 0:
  410.3 23.5 all-gather.1
where the time goes:
time: 718 us; the launch traced here: 710 us
  waiting for transfers between devices  224 us (31%)
  blocking collectives  146 us (20%)
  local copies, waits for them, and re-layouts  136 us (19%)
  matrix products  101 us (14%)
  other arithmetic  49.4 us (7%)
  starting transfers between devices  37.7 us (5%)
  between operations  15 us (2%)
    all_to_all x1, blocking collectives, local(): lax.all_to_all(outbound, ('seq', 'exp'), split_axis=0, concat_axis=0, til...  146 us
    all_to_all x1, waiting for transfers between devices, local(): lax.all_to_all(jnp.einsum('secf,efd->secd', hidden, down, preferred_eleme...  139 us
    ppermute x7, waiting for transfers between devices, from_behind(): return lax.ppermute(x, axis, pairs)  62.5 us
    pad x4, local copies, waits for them, and re-layouts, local(): lax.associative_scan(compose, (transition, written), axis=1)  34.2 us
    scatter x1, local copies, waits for them, and re-layouts, local(): jnp.zeros((experts_all * capacity, width), jnp.bfloat16).at[slot]  34.1 us
    ppermute x7, starting transfers between devices, from_behind(): return lax.ppermute(x, axis, pairs)  33.4 us
    unnamed x55, local copies, waits for them, and re-layouts  24.9 us
    all_gather x1, waiting for transfers between devices, local(): lax.all_gather(normed_mix, 'exp', axis=0, tiled=True)  22.1 us
  transfers between devices with their start and end apart: 9, of which 9 were waited for; matrix products, arithmetic and copies ran while one was open for 0% of the time, Pallas kernels for 0%

commit v1 on v0

v1 whole, which is shorter than its diff:
```python
from functools import partial

import jax
import jax.numpy as jnp
from jax import lax
from jax.experimental import pallas as pl
from jax.experimental.pallas import tpu as pltpu
from jax.sharding import PartitionSpec as P

CH = 128
VMEM_LIMIT = 56 * 1024 * 1024
BF = jnp.bfloat16
F32 = jnp.float32


def rms_scale(values, gain):
    wide = values.astype(F32)
    return wide * lax.rsqrt(jnp.mean(wide * wide, axis=-1, keepdims=True) + 1e-06) * gain


def dot(a, b):
    return jnp.dot(a, b, preferred_element_type=F32)


def split(a):
    high = a.astype(BF)
    return high, (a - high.astype(F32)).astype(BF)


def left_pair(a):
    high, low = split(a)
    return jnp.concatenate([high, low], axis=1)


def right_pair(b):
    high, low = split(b)
    row = jnp.concatenate([high, low], axis=1)
    return jnp.concatenate([row, row], axis=0)


def wide_product(a, b):
    columns = b.shape[1]
    both = dot(left_pair(a), right_pair(b))
    return both[:, :columns] + both[:, columns:]


def moe_kernel(capacity, first_ref, meta_ref, x_ref, gate_up_ref, down_ref, out_ref, rows_ref, back_ref):
    blocks, twice, tok = meta_ref.shape
    choose = twice // 2
    local_experts = gate_up_ref.shape[0]
    expert_width = down_ref.shape[1]
    pairs = blocks // 2
    pair_rows = rows_ref.shape[1] // pairs
    first = first_ref[0]
    matched, weights = [], []
    for block in range(blocks):
        ids = meta_ref[block, :choose, :]
        scale = meta_ref[block, choose:, :]
        for e in range(local_experts):
            hit = ids == (first + e).astype(F32)
            matched.append(jnp.max(jnp.where(hit, 1.0, 0.0), axis=0, keepdims=True))
            weights.append(jnp.sum(jnp.where(hit, scale, 0.0), axis=0, keepdims=True))
    match = jnp.concatenate(matched, axis=0)
    before = lax.broadcasted_iota(jnp.int32, (tok, tok), 0) < lax.broadcasted_iota(
        jnp.int32, (tok, tok), 1
    )
    rank = dot(match.astype(BF), jnp.where(before, 1.0, 0.0).astype(BF))
    rank = jnp.where(match > 0.5, rank, -1e4)
    row_number = lax.broadcasted_iota(jnp.int32, (pair_rows, 2 * tok), 0).astype(F32)
    picks = []
    for pair in range(pairs):
        x_pair = x_ref[pair * 2 * tok : (pair + 1) * 2 * tok, :]
        for e in range(local_experts):
            low = 2 * pair * local_experts + e
            high = low + local_experts
            place = jnp.concatenate(
                [rank[low : low + 1], rank[high : high + 1] + float(capacity)], axis=1
            )
            pick = jnp.where(row_number == place, 1.0, 0.0)
            picks.append(pick)
            rows_ref[e, pair * pair_rows : (pair + 1) * pair_rows, :] = dot(
                pick.astype(BF), x_pair
            ).astype(BF)
    for e in range(local_experts):
        both = dot(rows_ref[e], gate_up_ref[e])
        gate = both[:, :expert_width]
        hidden = (gate / (1.0 + jnp.exp(-gate)) * both[:, expert_width:]).astype(BF)
        back_ref[e] = dot(hidden, down_ref[e]).astype(BF)
    for pair in range(pairs):
        scaled, rows = [], []
        for e in range(local_experts):
            low = 2 * pair * local_experts + e
            high = low + local_experts
            weight = jnp.concatenate([weights[low], weights[high]], axis=1)
            scaled.append(picks[pair * local_experts + e] * weight)
            rows.append(back_ref[e, pair * pair_rows : (pair + 1) * pair_rows, :])
        high_part, low_part = split(jnp.concatenate(scaled, axis=0))
        left = jnp.concatenate([high_part, low_part], axis=0)
        right = jnp.concatenate(rows + rows, axis=0)
        out_ref[pair * 2 * tok : (pair + 1) * 2 * tok, :] = lax.dot_general(
            left, right, (((0,), (0,)), ((), ())), preferred_element_type=F32
        ).astype(BF)


def experts(gathered, meta, first, gate_up_weight, down, capacity):
    rows, width = gathered.shape
    blocks, twice, tok = meta.shape
    local_experts, _, double = gate_up_weight.shape
    group = min(8, blocks)
    pair_rows = -(-2 * capacity // 16) * 16
    held = group // 2 * pair_rows
    once = pl.Buffered(1)
    return pl.pallas_call(
        partial(moe_kernel, capacity),
        grid=(blocks // group,),
        in_specs=[
            pl.BlockSpec(memory_space=pltpu.SMEM),
            pl.BlockSpec((group, twice, tok), lambda i: (i, 0, 0)),
            pl.BlockSpec((group * tok, width), lambda i: (i, 0)),
            pl.BlockSpec(gate_up_weight.shape, lambda i: (0, 0, 0), pipeline_mode=once),
            pl.BlockSpec(down.shape, lambda i: (0, 0, 0), pipeline_mode=once),
        ],
        out_specs=pl.BlockSpec((group * tok, width), lambda i: (i, 0)),
        out_shape=jax.ShapeDtypeStruct((rows, width), BF),
        scratch_shapes=[
            pltpu.VMEM((local_experts, held, width), BF),
            pltpu.VMEM((local_experts, held, width), BF),
        ],
        compiler_params=pltpu.CompilerParams(vmem_limit_bytes=VMEM_LIMIT),
        cost_estimate=pl.CostEstimate(
            flops=2 * blocks * capacity * local_experts * width * double * 3 // 2,
            bytes_accessed=4 * rows * width + 2 * (gate_up_weight.size + down.size),
            transcendentals=0,
        ),
        name="experts",
    )(first, meta, gathered, gate_up_weight, down)


def unit_rows(values):
    return values * lax.rsqrt(jnp.sum(values * values, axis=-1, keepdims=True) + 1e-06)


def mixer_kernel(q_ref, k_ref, v_ref, sum_ref, rate_ref, enter_ref, local_ref, end_ref):
    length, dim = q_ref.shape[1:]
    blocks = length // CH
    span = range(blocks)
    rows = lax.broadcasted_iota(jnp.int32, (CH, CH), 0)
    columns = lax.broadcasted_iota(jnp.int32, (CH, CH), 1)
    strict = rows > columns
    inclusive = rows >= columns
    identity = jnp.where(rows == columns, 1.0, 0.0)
    cut = [slice(n * CH, (n + 1) * CH) for n in span]
    query = [unit_rows(q_ref[0, cut[n], :]) for n in span]
    key = [unit_rows(k_ref[0, cut[n], :]) for n in span]
    value = [v_ref[0, cut[n], :] for n in span]
    across = [jnp.broadcast_to(sum_ref[0, n : n + 1, :], (CH, CH)) for n in span]
    down_rows = [across[n].T for n in span]
    rate = [jnp.broadcast_to(rate_ref[0, n : n + 1, :], (CH, CH)).T for n in span]
    fade = [jnp.exp(jnp.where(inclusive, down_rows[n] - across[n], 0.0)) for n in span]
    growth = [jnp.exp(down_rows[n]) for n in span]
    last = [jnp.broadcast_to(down_rows[n][CH - 1 : CH, :], (CH, CH)) for n in span]
    remaining = [jnp.exp(last[n] - down_rows[n]) for n in span]
    whole = [jnp.exp(last[n]) for n in span]
    both = []
    for n in span:
        high, low = split(key[n])
        left = jnp.concatenate(
            [jnp.concatenate([high, low], axis=1), left_pair(query[n])], axis=0
        )
        hh = jnp.concatenate([high, high], axis=1)
        ll = jnp.concatenate([low, low], axis=1)
        right_t = jnp.concatenate([hh, ll], axis=0)
        got = lax.dot_general(left, right_t, (((1,), (1,)), ((), ())), preferred_element_type=F32)
        both.append(got[:, :CH] + got[:, CH:])
    lower = [jnp.where(strict, rate[n] * fade[n] * both[n][:CH], 0.0) for n in span]
    masked = [jnp.where(inclusive, fade[n] * both[n][CH:], 0.0) for n in span]

    def ring(size):
        shared = (rows // (2 * size)) == (columns // (2 * size))
        return shared & (rows // size % 2 == 1) & (columns // size % 2 == 0)

    inverse = [identity - jnp.where(ring(1), lower[n], 0.0) for n in span]
    size = 2
    while size < CH:
        here = ring(size)
        step = [wide_product(jnp.where(here, lower[n], 0.0), inverse[n]) for n in span]
        inverse = [inverse[n] - wide_product(inverse[n], step[n]) for n in span]
        size *= 2
    solved = [
        wide_product(
            inverse[n],
            jnp.concatenate([rate[n] * growth[n] * key[n], rate[n] * value[n]], axis=1),
        )
        for n in span
    ]
    ended = [wide_product((remaining[n] * key[n]).T, solved[n]) for n in span]
    probed = [wide_product(masked[n], solved[n]) for n in span]
    state = None
    for n in span:
        entering = growth[n] * query[n] - probed[n][:, :dim]
        output = probed[n][:, dim:]
        transition = whole[n] * identity - ended[n][:, :dim]
        written = ended[n][:, dim:]
        if n == 0:
            state = jnp.concatenate([transition, written], axis=1)
        else:
            moved = wide_product(jnp.concatenate([entering, transition], axis=0), state)
            entering = moved[:CH, :dim]
            output = output + moved[:CH, dim:]
            state = jnp.concatenate([moved[CH:, :dim], moved[CH:, dim:] + written], axis=1)
        enter_ref[cut[n], :] = entering
        local_ref[cut[n], :] = output
    end_ref[0] = state


def mixer(projected, sums, rates):
    _, length, columns = projected.shape
    heads, blocks, _ = sums.shape
    dim = columns // heads
    part = lambda p: pl.BlockSpec((1, length, dim), lambda h, p=p: (p, 0, h))
    per_head = pl.BlockSpec((1, blocks, CH), lambda h: (h, 0, 0))
    per_column = pl.BlockSpec((length, dim), lambda h: (0, h))
    return pl.pallas_call(
        mixer_kernel,
        grid=(heads,),
        in_specs=[part(0), part(1), part(2), per_head, per_head],
        out_specs=[per_column, per_column, pl.BlockSpec((1, dim, 2 * dim), lambda h: (h, 0, 0))],
        out_shape=[
            jax.ShapeDtypeStruct((length, columns), F32),
            jax.ShapeDtypeStruct((length, columns), F32),
            jax.ShapeDtypeStruct((heads, dim, 2 * dim), F32),
        ],
        compiler_params=pltpu.CompilerParams(vmem_limit_bytes=VMEM_LIMIT),
        name="mixer",
    )(projected, projected, projected, sums, rates)


def carry_kernel(ends_ref, states_ref):
    segments, dim, _ = ends_ref.shape
    state = jnp.zeros((dim, dim), F32)
    for s in range(segments):
        states_ref[s] = state
        if s < segments - 1:
            state = wide_product(ends_ref[s, :, :dim], state) + ends_ref[s, :, dim:]


def carry(ends):
    segments, dim, _ = ends.shape
    return pl.pallas_call(
        carry_kernel,
        out_shape=jax.ShapeDtypeStruct((segments, dim, dim), F32),
        compiler_params=pltpu.CompilerParams(vmem_limit_bytes=VMEM_LIMIT),
        name="carry",
    )(ends)


def finish_kernel(enter_ref, local_ref, state_ref, core_ref):
    core_ref[...] = local_ref[...] + wide_product(enter_ref[...], state_ref[0])


def finish(entering, local_out, states):
    length, columns = entering.shape
    heads, dim, _ = states.shape
    per_column = pl.BlockSpec((length, dim), lambda h: (0, h))
    return pl.pallas_call(
        finish_kernel,
        grid=(heads,),
        in_specs=[per_column, per_column, pl.BlockSpec((1, dim, dim), lambda h: (h, 0, 0))],
        out_specs=per_column,
        out_shape=jax.ShapeDtypeStruct((length, columns), F32),
        compiler_params=pltpu.CompilerParams(vmem_limit_bytes=VMEM_LIMIT),
        name="finish",
    )(entering, local_out, states)


def relay(ends, seq_count):
    dim = ends.shape[1]
    pairs = [(i, i + 1) for i in range(seq_count - 1)]

    def step(_, incoming):
        outgoing = (
            jnp.einsum("hij,hjk->hik", ends[..., :dim], incoming, precision=lax.Precision.HIGHEST)
            + ends[..., dim:]
        )
        return lax.ppermute(outgoing, "seq", pairs)

    return lax.fori_loop(0, seq_count - 1, step, jnp.zeros_like(ends[..., :dim]))


def route_all(normed, expert_ids, expert_weights, gate_up_weight, down, capacity):
    axes = ("seq", "exp")
    tok_rows = normed.shape[0]
    me = lax.axis_index("seq") * lax.axis_size("exp") + lax.axis_index("exp")
    first = (me * gate_up_weight.shape[0]).astype(jnp.int32).reshape(1)
    meta = jnp.concatenate([expert_ids.astype(F32).T, expert_weights.T], axis=0)
    meta = lax.all_gather(meta, axes, axis=0, tiled=False)
    gathered = lax.all_gather(normed, axes, axis=0, tiled=True)
    partial_sums = experts(gathered, meta, first, gate_up_weight, down, capacity)
    return lax.psum_scatter(partial_sums, axes, scatter_dimension=0, tiled=True).astype(F32)


def route_some(normed, expert_ids, expert_weights, gate_up_weight, down, capacity):
    axes = ("seq", "exp")
    tok_rows, width = normed.shape
    choose = expert_ids.shape[1]
    local_experts = gate_up_weight.shape[0]
    expert_width = down.shape[1]
    devices = lax.axis_size("seq") * lax.axis_size("exp")
    experts_all = local_experts * devices
    flat_ids = expert_ids.reshape(-1)
    onehot = (flat_ids[:, None] == jnp.arange(experts_all, dtype=jnp.int32)[None, :]).astype(
        jnp.int32
    )
    rank = jnp.sum(jnp.cumsum(onehot, axis=0) * onehot, axis=1) - 1
    slot = flat_ids * capacity + rank
    token_of = jnp.arange(tok_rows * choose, dtype=jnp.int32) // choose
    send = jnp.zeros((experts_all * capacity, width), BF).at[slot].set(normed[token_of])
    both = jnp.einsum(
        "secd,edf->secf",
        lax.all_to_all(
            send.reshape(devices, local_experts, capacity, width),
            axes,
            split_axis=0,
            concat_axis=0,
            tiled=True,
        ),
        gate_up_weight,
        preferred_element_type=F32,
    )
    hidden = (jax.nn.silu(both[..., :expert_width]) * both[..., expert_width:]).astype(BF)
    back = lax.all_to_all(
        jnp.einsum("secf,efd->secd", hidden, down, preferred_element_type=F32).astype(BF),
        axes,
        split_axis=0,
        concat_axis=0,
        tiled=True,
    )
    back_rows = back.reshape(experts_all * capacity, width)[slot].astype(F32)
    return jnp.sum(
        back_rows.reshape(tok_rows, choose, width) * expert_weights[:, :, None], axis=1
    )


def local(
    stream,
    moe_gain,
    expert_ids,
    expert_weights,
    gate_up_weight,
    down,
    mixer_gain,
    qkv_weight,
    decay_log,
    write_rate,
):
    tok_rows, width = stream.shape
    choose = expert_ids.shape[1]
    seq_count = lax.axis_size("seq")
    devices = seq_count * lax.axis_size("exp")
    experts_all = gate_up_weight.shape[0] * devices
    capacity = max(2, (tok_rows * choose * 6 + experts_all * 5 - 1) // (experts_all * 5))
    normed = rms_scale(stream, moe_gain).astype(BF)
    route = route_all if devices * tok_rows * width * 4 <= 40 * 2**20 else route_some
    moe = route(normed, expert_ids, expert_weights, gate_up_weight, down, capacity)
    mixed = (stream.astype(F32) + moe).astype(BF)
    normed_mix = rms_scale(mixed, mixer_gain).astype(BF)
    projected = jnp.einsum(
        "rd,pde->pre",
        lax.all_gather(normed_mix, "exp", axis=0, tiled=True),
        qkv_weight,
        preferred_element_type=F32,
    )
    length = projected.shape[1]
    heads = decay_log.shape[1]
    blocks = length // CH
    sums = jnp.cumsum(decay_log.T.reshape(heads, blocks, CH), axis=-1)
    rates = write_rate.T.reshape(heads, blocks, CH)
    entering, local_out, ends = mixer(projected, sums, rates)
    if heads % seq_count == 0:
        dim = ends.shape[1]
        each = heads // seq_count
        held = lax.all_to_all(ends, "seq", split_axis=0, concat_axis=0, tiled=True)
        held = held.reshape(seq_count, each, dim, 2 * dim)
        states = jnp.stack([carry(held[:, i]) for i in range(each)], axis=1)
        arriving = lax.all_to_all(
            states.reshape(seq_count * each, dim, dim), "seq", split_axis=0, concat_axis=0, tiled=True
        )
    else:
        arriving = relay(ends, seq_count)
    return (mixed, finish(entering, local_out, arriving))


def solution(mesh):
    in_specs = (
        P(("seq", "exp"), None),
        P(),
        P(("seq", "exp"), None),
        P(("seq", "exp"), None),
        P(("seq", "exp"), None, None),
        P(("seq", "exp"), None, None),
        P(),
        P(None, None, "exp"),
        P("seq", "exp"),
        P("seq", "exp"),
    )
    out_specs = (P(("seq", "exp"), None), P("seq", "exp"))
    return jax.shard_map(local, mesh=mesh, in_specs=in_specs, out_specs=out_specs, check_vma=False)
```

time: 718 us -> 482 us (0.67); the launches traced: 710 us -> 481 us
  local copies, waits for them, and re-layouts: 136 us -> 1.24 us
  matrix products: 101 us -> 12 us
  Pallas kernels: 0 us -> 75.3 us
  waiting for transfers between devices: 224 us -> 273 us
  blocking collectives: 146 us -> 98 us
  other arithmetic: 49.4 us -> 8.12 us
  starting transfers between devices: 37.7 us -> 0.12 us
    reduce_scatter x0 -> x1, waiting for transfers between devices: none -> 181 us  [route_all(): lax.psum_scatter(partial_sums, axes, scatter_dimension=0, tiled=True)]
    all_to_all x1 -> x0, waiting for transfers between devices: 139 us -> none  [local(): lax.all_to_all(jnp.einsum('secf,efd->secd', hidden, down, preferred_eleme...]
    all_to_all x1 -> x2, blocking collectives: 146 us -> 49.9 us  [the longest x1 31.7 us: local(): held = lax.all_to_all(ends, 'seq', split_axis=0, concat_axis=0, tiled=True)]
    dot_general x37 -> x0, matrix products: 91.1 us -> none  [the longest x6 15 us: local(): inverse = inverse + product('hnij,hnjk->hnik', inverse, power)]
    pallas_call x0 -> x4, Pallas kernels: none -> 75.3 us  [the longest x1 35.3 us: mixer(): pl.pallas_call(mixer_kernel, grid=(heads,), in_specs=[part(0), part(1), p...]
    all_gather x0 -> x1, waiting for transfers between devices: none -> 69.4 us  [route_all(): gathered = lax.all_gather(normed, axes, axis=0, tiled=True)]
    ppermute x7 -> x0, waiting for transfers between devices: 62.5 us -> none  [from_behind(): return lax.ppermute(x, axis, pairs)]
    all_gather x0 -> x1, blocking collectives: none -> 48.1 us  [route_all(): meta = lax.all_gather(meta, axes, axis=0, tiled=False)]
  transfers between devices with their start and end apart: 9 -> 3, of which waited for: 9 -> 3; matrix products, arithmetic and copies ran while one was open for 0% -> 1% of each run, Pallas kernels for 0% -> 0%
where the time goes in v1:
time: 482 us; the launch traced here: 481 us
  waiting for transfers between devices  273 us (57%)
  blocking collectives  98 us (20%)
  Pallas kernels  75.3 us (16%)
  between operations  13.8 us (3%)
  matrix products  12 us (2%)
  other arithmetic  8.12 us (2%)
    reduce_scatter x1, waiting for transfers between devices, route_all(): lax.psum_scatter(partial_sums, axes, scatter_dimension=0, tiled=True)  181 us
    all_gather x1, waiting for transfers between devices, route_all(): gathered = lax.all_gather(normed, axes, axis=0, tiled=True)  69.4 us
    all_gather x1, blocking collectives, route_all(): meta = lax.all_gather(meta, axes, axis=0, tiled=False)  48.1 us
    pallas_call x1, Pallas kernels, mixer(): pl.pallas_call(mixer_kernel, grid=(heads,), in_specs=[part(0), part(1), p...  35.3 us
    all_to_all x1, blocking collectives, local(): held = lax.all_to_all(ends, 'seq', split_axis=0, concat_axis=0, tiled=True)  31.7 us
    pallas_call x1, Pallas kernels, experts(): pl.pallas_call(partial(moe_kernel, capacity), grid=(blocks // group,), in...  30 us
    all_gather x1, waiting for transfers between devices, local(): lax.all_gather(normed_mix, 'exp', axis=0, tiled=True)  22 us
    all_to_all x1, blocking collectives, local(): lax.all_to_all(states.reshape(seq_count * each, dim, dim), 'seq', split_a...  18.2 us
  transfers between devices with their start and end apart: 3, of which 3 were waited for; matrix products, arithmetic and copies ran while one was open for 1% of the time, Pallas kernels for 0%

profile of v1, /device:TPU:0, one launch (start us, length us, event | category | flops | bytes accessed | tf_op | source)
XLA Modules:
  0.0 481.3 jit_solution(13957394519269130112)
XLA Ops:
  7.2 0.0 all-gather.5.cloned.1.call-start
  7.2 1.2 fusion.4
  8.4 2.0 fusion.6
  10.5 0.0 all-gather.5.cloned.1.call-update
  10.5 0.0 reduce-scatter.2.cloned.1.call-start
  10.6 0.7 convert_bitcast_fusion
  11.3 0.7 maximum_bitcast_fusion
  12.0 48.1 %all-gather.1.meta_ref = f32[32,20,128]{2,1,0:T(8,128)} all-gather(f32[1,20,128]{2,1,0:T(8,128)S(1)} %maximum_bitcast_fusion), channel_id=2, replica_groups=mesh['seq'=8,'exp'=4] {'seq','exp'}, dimensions={0}, use_global_device_ids=true | all-gather | bytes 337920 | tf_op jit(solution)/shard_map/all_gather | solution.py:296
  60.1 69.4 %all-gather.5.cloned.1.call-done.x_ref = bf16[4096,2048]{1,0:T(8,128)(2,1)} async-done(((bf16[128,2048]{1,0:T(8,128)(2,1)}), bf16[4096,2048]{1,0:T(8,128)(2,1)}) %all-gather.5.cloned.1.call-update) | async-done | bytes 16777232 | tf_op jit(solution)/shard_map/all_gather | solution.py:297
  129.5 30.0 %experts.1 = bf16[4096,2048]{1,0:T(8,128)(2,1)} custom-call(s32[1]{0:T(128)} %bitcast.first_ref, f32[32,20,128]{2,1,0:T(8,128)} %all-gather.1.meta_ref, bf16[4096,2048]{1,0:T(8,128)(2,1)} %all-gather.5.cloned.1.call-done.x_ref, bf16[2,2048,1024]{2,1,0:T(8,128)(2,1)} %gate_up_ref.1, bf16[2,512,2048]{2,1,0:T(8,128)(2,1)} %down_ref.1), custom_call_target="tpu_custom_call" | custom-call | flops 9663676416 | bytes 46137344 | tf_op jit(solution)/shard_map/experts/pallas_call | solution.py:113
  159.5 0.0 copy-start.3
  159.5 0.0 reduce-scatter.2.cloned.1.call-update
  159.5 0.0 all-gather.7.cloned.1.call-start
  159.5 181.3 %reduce-scatter.2.cloned.1.call-done = bf16[128,2048]{1,0:T(8,128)(2,1)} async-done(((bf16[4096,2048]{1,0:T(8,128)(2,1)}), bf16[128,2048]{1,0:T(8,128)(2,1)}) %reduce-scatter.2.cloned.1.call-update) | async-done | bytes 524304 | tf_op jit(solution)/shard_map/reduce_scatter | solution.py:299
  340.8 0.0 copy-done
  340.8 1.3 fusion.1
  342.1 0.0 copy-done.4
  342.1 1.0 fusion.3
  343.1 0.0 all-gather.7.cloned.1.call-update
  343.2 0.0 copy-done.2
  343.2 1.1 reduce_window_sum.11
  344.3 0.6 copy.13.sum_ref
  344.9 0.0 copy-done.3
  344.9 0.6 reshape.33.rate_ref
  345.5 22.0 %all-gather.7.cloned.1.call-done = bf16[512,2048]{1,0:T(8,128)(2,1)} async-done(((bf16[128,2048]{1,0:T(8,128)(2,1)}), bf16[512,2048]{1,0:T(8,128)(2,1)}) %all-gather.7.cloned.1.call-update) | async-done | bytes 2097168 | tf_op jit(solution)/shard_map/all_gather | solution.py:369
  367.5 12.0 %convolution_bitcast_fusion.q_ref.k_ref.v_ref = f32[3,512,1024]{2,1,0:T(8,128)} fusion(bf16[3,2048,1024]{2,1,0:T(8,128)(2,1)} %param.17, bf16[512,2048]{1,0:T(8,128)(2,1)} %all-gather.7.cloned.1.call-done), kind=kOutput, calls=%fused_computation | convolution fusion | flops 6442450944 | bytes 20971520 | tf_op jit(solution)/shard_map/rd,pde->pre/dot_general | solution.py:367
  379.5 0.0 copy-done.1
  379.5 35.3 %mixer.1 = (f32[512,1024]{1,0:T(8,128)}, f32[512,1024]{1,0:T(8,128)}, f32[8,128,256]{2,1,0:T(8,128)}) custom-call(f32[3,512,1024]{2,1,0:T(8,128)} %convolution_bitcast_fusion.q_ref.k_ref.v_ref, f32[3,512,1024]{2,1,0:T(8,128)} %convolution_bitcast_fusion.q_ref.k_ref.v_ref, f32[3,512,1024]{2,1,0:T(8,128)} %convolution_bitcast_fusion.q_ref.k_ref.v_ref, ...), custom_call_target="tpu_custom_call" | custom-call | tf_op jit(solution)/shard_map/mixer/pallas_call | solution.py:223
  414.7 31.7 %all_to_all.10.ends_ref = f32[8,128,256]{2,1,0:T(8,128)} all-to-all(f32[8,128,256]{2,1,0:T(8,128)} %get-tuple-element.7), channel_id=1, replica_groups=mesh['seq'=8,'exp'=4] {'seq'}, dimensions={0} | all-to-all | bytes 2097152 | tf_op jit(solution)/shard_map/all_to_all | solution.py:382
  446.5 3.2 carry.1
  449.7 18.2 %all_to_all.11.state_ref = f32[8,128,128]{2,1,0:T(8,128)} all-to-all(f32[8,128,128]{2,1,0:T(8,128)} %carry.1), channel_id=1, replica_groups=mesh['seq'=8,'exp'=4] {'seq'}, dimensions={0} | all-to-all | bytes 1048576 | tf_op jit(solution)/shard_map/all_to_all | solution.py:385
  467.9 6.9 %finish.1 = f32[512,1024]{1,0:T(8,128)} custom-call(f32[512,1024]{1,0:T(8,128)} %get-tuple-element.5.enter_ref, f32[512,1024]{1,0:T(8,128)} %get-tuple-element.6.local_ref, f32[8,128,128]{2,1,0:T(8,128)} %all_to_all.11.state_ref), custom_call_target="tpu_custom_call" | custom-call | tf_op jit(solution)/shard_map/finish/pallas_call | solution.py:265
  (6 shorter events, 0.0 us)
Async XLA Ops:
  7.2 122.3 %all-gather.5.cloned.1.call-start = ((), (), s32[]{:S(2)}) async-start(), calls=%async_computation.3 | async-start | bytes 17301504 | tf_op jit(solution)/shard_map/all_gather | solution.py:297
  10.5 330.3 %reduce-scatter.2.cloned.1.call-start = ((), (), s32[]{:S(2)}) async-start(), calls=%async_computation.4 | async-start | bytes 17301504 | tf_op jit(solution)/shard_map/reduce_scatter | solution.py:299
  159.4 181.4 %copy-start = (bf16[128,2048]{1,0:T(8,128)(2,1)S(1)}, bf16[128,2048]{1,0:T(8,128)(2,1)}, u32[]{:S(2)}) copy-start(bf16[128,2048]{1,0:T(8,128)(2,1)} %param.10) | copy-start | bytes 1572868
  159.4 182.7 %copy-start.4 = (f32[2048]{0:T(1024)S(1)}, f32[2048]{0:T(1024)}, u32[]{:S(2)}) copy-start(f32[2048]{0:T(1024)} %param.16) | copy-start | bytes 24580
  159.4 183.7 %copy-start.2 = (f32[512,8]{0,1:T(8,128)S(1)}, f32[512,8]{0,1:T(8,128)}, u32[]{:S(2)}) copy-start(f32[512,8]{0,1:T(8,128)} %param.18) | copy-start | bytes 49156
  159.5 185.5 %copy-start.3 = (f32[512,8]{0,1:T(8,128)S(1)}, f32[512,8]{0,1:T(8,128)}, u32[]{:S(2)}) copy-start(f32[512,8]{0,1:T(8,128)} %param.19) | copy-start | bytes 49156
  159.5 208.0 %all-gather.7.cloned.1.call-start = ((), (), s32[]{:S(2)}) async-start(), calls=%async_computation.5 | async-start | bytes 2621440 | tf_op jit(solution)/shard_map/all_gather | solution.py:369
  342.1 37.4 %copy-start.1 = (bf16[128,2048]{1,0:T(8,128)(2,1)}, bf16[128,2048]{1,0:T(8,128)(2,1)S(1)}, u32[]{:S(2)}) copy-start(bf16[128,2048]{1,0:T(8,128)(2,1)S(1)} %get-tuple-element.9) | copy-start | bytes 1572868
Sparse Core Ops, SparseCore 0:
  11.4 117.9 all-gather.4
  159.6 181.1 reduce-scatter.1
  343.3 24.1 all-gather.6

commit v2 on v1

--- a/solution.py
+++ b/solution.py
@@ -8,6 +8,7 @@
 from jax.sharding import PartitionSpec as P
 
 CH = 128
+ROUTE_STEP = 16
 VMEM_LIMIT = 56 * 1024 * 1024
 BF = jnp.bfloat16
 F32 = jnp.float32
@@ -44,20 +45,40 @@
     return both[:, :columns] + both[:, columns:]
 
 
-def moe_kernel(capacity, first_ref, meta_ref, x_ref, gate_up_ref, down_ref, out_ref, rows_ref, back_ref):
-    blocks, twice, tok = meta_ref.shape
-    choose = twice // 2
-    local_experts = gate_up_ref.shape[0]
+def moe_kernel(capacity, choose, *refs):
+    first_ref, *block_refs = refs[:5]
+    weight_refs = refs[5:9]
+    out_refs = refs[9:13]
+    gate_up_ref, down_ref, rows_ref, back_ref, sem = refs[13:]
+    tok, wide = block_refs[0].shape
+    width = rows_ref.shape[2]
+    experts_here = gate_up_ref.shape[0]
+    half = experts_here // 2
     expert_width = down_ref.shape[1]
-    pairs = blocks // 2
-    pair_rows = rows_ref.shape[1] // pairs
-    first = first_ref[0]
+    pair_rows = rows_ref.shape[1] // 2
+
+    copies = []
+    for e in range(experts_here):
+        side, at = divmod(e, half)
+        fetch_in = pltpu.make_async_copy(
+            weight_refs[2 * side].at[at], gate_up_ref.at[e], sem.at[0, e]
+        )
+        fetch_out = pltpu.make_async_copy(
+            weight_refs[2 * side + 1].at[at], down_ref.at[e], sem.at[1, e]
+        )
+        fetch_in.start()
+        fetch_out.start()
+        copies.append((fetch_in, fetch_out))
+
     matched, weights = [], []
-    for block in range(blocks):
-        ids = meta_ref[block, :choose, :]
-        scale = meta_ref[block, choose:, :]
-        for e in range(local_experts):
-            hit = ids == (first + e).astype(F32)
+    for block_ref in block_refs:
+        routing = block_ref[:, width:].astype(F32).T
+        ids = routing[:choose]
+        scale = routing[ROUTE_STEP : ROUTE_STEP + choose]
+        scale = scale + routing[2 * ROUTE_STEP : 2 * ROUTE_STEP + choose]
+        for e in range(experts_here):
+            side, at = divmod(e, half)
+            hit = ids == (first_ref[side] + at).astype(F32)
             matched.append(jnp.max(jnp.where(hit, 1.0, 0.0), axis=0, keepdims=True))
             weights.append(jnp.sum(jnp.where(hit, scale, 0.0), axis=0, keepdims=True))
     match = jnp.concatenate(matched, axis=0)
@@ -68,72 +89,78 @@
     rank = jnp.where(match > 0.5, rank, -1e4)
     row_number = lax.broadcasted_iota(jnp.int32, (pair_rows, 2 * tok), 0).astype(F32)
     picks = []
-    for pair in range(pairs):
-        x_pair = x_ref[pair * 2 * tok : (pair + 1) * 2 * tok, :]
-        for e in range(local_experts):
-            low = 2 * pair * local_experts + e
-            high = low + local_experts
+    for pair in range(2):
+        x_pair = jnp.concatenate(
+            [block_refs[2 * pair][:, :width], block_refs[2 * pair + 1][:, :width]], axis=0
+        )
+        here = []
+        for e in range(experts_here):
+            low = 2 * pair * experts_here + e
+            high = low + experts_here
             place = jnp.concatenate(
                 [rank[low : low + 1], rank[high : high + 1] + float(capacity)], axis=1
             )
-            pick = jnp.where(row_number == place, 1.0, 0.0)
-            picks.append(pick)
-            rows_ref[e, pair * pair_rows : (pair + 1) * pair_rows, :] = dot(
-                pick.astype(BF), x_pair
-            ).astype(BF)
-    for e in range(local_experts):
+            here.append(jnp.where(row_number == place, 1.0, 0.0))
+        picks.append(here)
+        chosen = dot(jnp.concatenate(here, axis=0).astype(BF), x_pair).astype(BF)
+        for e in range(experts_here):
+            rows_ref[e, pair * pair_rows : (pair + 1) * pair_rows, :] = chosen[
+                e * pair_rows : (e + 1) * pair_rows
+            ]
+    for e in range(experts_here):
+        copies[e][0].wait()
         both = dot(rows_ref[e], gate_up_ref[e])
         gate = both[:, :expert_width]
         hidden = (gate / (1.0 + jnp.exp(-gate)) * both[:, expert_width:]).astype(BF)
+        copies[e][1].wait()
         back_ref[e] = dot(hidden, down_ref[e]).astype(BF)
-    for pair in range(pairs):
+    for pair in range(2):
         scaled, rows = [], []
-        for e in range(local_experts):
-            low = 2 * pair * local_experts + e
-            high = low + local_experts
+        for e in range(experts_here):
+            low = 2 * pair * experts_here + e
+            high = low + experts_here
             weight = jnp.concatenate([weights[low], weights[high]], axis=1)
-            scaled.append(picks[pair * local_experts + e] * weight)
+            scaled.append(picks[pair][e] * weight)
             rows.append(back_ref[e, pair * pair_rows : (pair + 1) * pair_rows, :])
         high_part, low_part = split(jnp.concatenate(scaled, axis=0))
         left = jnp.concatenate([high_part, low_part], axis=0)
         right = jnp.concatenate(rows + rows, axis=0)
-        out_ref[pair * 2 * tok : (pair + 1) * 2 * tok, :] = lax.dot_general(
+        summed = lax.dot_general(
             left, right, (((0,), (0,)), ((), ())), preferred_element_type=F32
         ).astype(BF)
-
-
-def experts(gathered, meta, first, gate_up_weight, down, capacity):
-    rows, width = gathered.shape
-    blocks, twice, tok = meta.shape
-    local_experts, _, double = gate_up_weight.shape
-    group = min(8, blocks)
+        out_refs[2 * pair][...] = summed[:tok]
+        out_refs[2 * pair + 1][...] = summed[tok:]
+
+
+def experts(blocks, first, weights, capacity, choose):
+    tok, wide = blocks[0].shape
+    gate_up_weight, down = weights[:2]
+    local_experts, width, double = gate_up_weight.shape
+    here = 2 * local_experts
     pair_rows = -(-2 * capacity // 16) * 16
-    held = group // 2 * pair_rows
-    once = pl.Buffered(1)
+    whole = pl.BlockSpec(memory_space=pltpu.VMEM)
     return pl.pallas_call(
-        partial(moe_kernel, capacity),
-        grid=(blocks // group,),
-        in_specs=[
-            pl.BlockSpec(memory_space=pltpu.SMEM),
-            pl.BlockSpec((group, twice, tok), lambda i: (i, 0, 0)),
-            pl.BlockSpec((group * tok, width), lambda i: (i, 0)),
-            pl.BlockSpec(gate_up_weight.shape, lambda i: (0, 0, 0), pipeline_mode=once),
-            pl.BlockSpec(down.shape, lambda i: (0, 0, 0), pipeline_mode=once),
-        ],
-        out_specs=pl.BlockSpec((group * tok, width), lambda i: (i, 0)),
-        out_shape=jax.ShapeDtypeStruct((rows, width), BF),
+        partial(moe_kernel, capacity, choose),
+        in_specs=[pl.BlockSpec(memory_space=pltpu.SMEM)]
+        + [whole] * 4
+        + [pl.BlockSpec(memory_space=pl.ANY)] * 4,
+        out_specs=[whole] * 4,
+        out_shape=[jax.ShapeDtypeStruct((tok, width), BF)] * 4,
         scratch_shapes=[
-            pltpu.VMEM((local_experts, held, width), BF),
-            pltpu.VMEM((local_experts, held, width), BF),
+            pltpu.VMEM((here,) + gate_up_weight.shape[1:], BF),
+            pltpu.VMEM((here,) + down.shape[1:], BF),
+            pltpu.VMEM((here, 2 * pair_rows, width), BF),
+            pltpu.VMEM((here, 2 * pair_rows, width), BF),
+            pltpu.SemaphoreType.DMA((2, here)),
         ],
         compiler_params=pltpu.CompilerParams(vmem_limit_bytes=VMEM_LIMIT),
         cost_estimate=pl.CostEstimate(
-            flops=2 * blocks * capacity * local_experts * width * double * 3 // 2,
-            bytes_accessed=4 * rows * width + 2 * (gate_up_weight.size + down.size),
+            flops=2 * here * 2 * pair_rows * width * double * 3,
+            bytes_accessed=4 * (gate_up_weight.size + down.size),
             transcendentals=0,
         ),
         name="experts",
-    )(first, meta, gathered, gate_up_weight, down)
+    )(first, *blocks, *weights)
 
 
 def unit_rows(values):
@@ -196,6 +223,7 @@
     ended = [wide_product((remaining[n] * key[n]).T, solved[n]) for n in span]
     probed = [wide_product(masked[n], solved[n]) for n in span]
     state = None
+    total_decay = None
     for n in span:
         entering = growth[n] * query[n] - probed[n][:, :dim]
         output = probed[n][:, dim:]
@@ -203,14 +231,18 @@
         written = ended[n][:, dim:]
         if n == 0:
             state = jnp.concatenate([transition, written], axis=1)
+            total_decay = whole[n]
         else:
             moved = wide_product(jnp.concatenate([entering, transition], axis=0), state)
             entering = moved[:CH, :dim]
             output = output + moved[:CH, dim:]
             state = jnp.concatenate([moved[CH:, :dim], moved[CH:, dim:] + written], axis=1)
+            total_decay = total_decay * whole[n]
         enter_ref[cut[n], :] = entering
         local_ref[cut[n], :] = output
-    end_ref[0] = state
+    end_ref[0, :dim, :dim] = (total_decay * identity - state[:, :dim]).astype(BF)
+    end_ref[0, :dim, dim:] = state[:, dim:].astype(BF)
+    end_ref[0, dim:, :] = left_pair(total_decay[:16])
 
 
 def mixer(projected, sums, rates):
@@ -224,11 +256,11 @@
         mixer_kernel,
         grid=(heads,),
         in_specs=[part(0), part(1), part(2), per_head, per_head],
-        out_specs=[per_column, per_column, pl.BlockSpec((1, dim, 2 * dim), lambda h: (h, 0, 0))],
+        out_specs=[per_column, per_column, pl.BlockSpec((1, dim + 16, 2 * dim), lambda h: (h, 0, 0))],
         out_shape=[
             jax.ShapeDtypeStruct((length, columns), F32),
             jax.ShapeDtypeStruct((length, columns), F32),
-            jax.ShapeDtypeStruct((heads, dim, 2 * dim), F32),
+            jax.ShapeDtypeStruct((heads, dim + 16, 2 * dim), BF),
         ],
         compiler_params=pltpu.CompilerParams(vmem_limit_bytes=VMEM_LIMIT),
         name="mixer",
@@ -236,26 +268,34 @@
 
 
 def carry_kernel(ends_ref, states_ref):
-    segments, dim, _ = ends_ref.shape
+    segments, _, double = ends_ref.shape
+    dim = double // 2
     state = jnp.zeros((dim, dim), F32)
     for s in range(segments):
-        states_ref[s] = state
+        states_ref[s] = state.astype(BF)
         if s < segments - 1:
-            state = wide_product(ends_ref[s, :, :dim], state) + ends_ref[s, :, dim:]
+            decay = ends_ref[s, dim : dim + 1, :].astype(F32)
+            decay = decay[:, :dim] + decay[:, dim:]
+            removed = dot(ends_ref[s, :dim, :dim], left_pair(state))
+            removed = removed[:, :dim] + removed[:, dim:]
+            state = decay * state - removed + ends_ref[s, :dim, dim:].astype(F32)
 
 
 def carry(ends):
-    segments, dim, _ = ends.shape
+    segments, _, double = ends.shape
     return pl.pallas_call(
         carry_kernel,
-        out_shape=jax.ShapeDtypeStruct((segments, dim, dim), F32),
+        out_shape=jax.ShapeDtypeStruct((segments, double // 2, double // 2), BF),
         compiler_params=pltpu.CompilerParams(vmem_limit_bytes=VMEM_LIMIT),
         name="carry",
     )(ends)
 
 
 def finish_kernel(enter_ref, local_ref, state_ref, core_ref):
-    core_ref[...] = local_ref[...] + wide_product(enter_ref[...], state_ref[0])
+    state = state_ref[0]
+    core_ref[...] = local_ref[...] + dot(
+        left_pair(enter_ref[...]), jnp.concatenate([state, state], axis=0)
+    )
 
 
 def finish(entering, local_out, states):
@@ -274,29 +314,85 @@
 
 
 def relay(ends, seq_count):
-    dim = ends.shape[1]
+    dim = ends.shape[2] // 2
     pairs = [(i, i + 1) for i in range(seq_count - 1)]
+    removed, written = ends[:, :dim, :dim].astype(F32), ends[:, :dim, dim:].astype(F32)
+    decay = ends[:, dim, :1].astype(F32) + ends[:, dim, dim : dim + 1].astype(F32)
 
     def step(_, incoming):
-        outgoing = (
-            jnp.einsum("hij,hjk->hik", ends[..., :dim], incoming, precision=lax.Precision.HIGHEST)
-            + ends[..., dim:]
+        outgoing = decay[:, :, None] * incoming + written
+        outgoing = outgoing - jnp.einsum(
+            "hij,hjk->hik", removed, incoming, precision=lax.Precision.HIGHEST
         )
         return lax.ppermute(outgoing, "seq", pairs)
 
-    return lax.fori_loop(0, seq_count - 1, step, jnp.zeros_like(ends[..., :dim]))
-
-
-def route_all(normed, expert_ids, expert_weights, gate_up_weight, down, capacity):
-    axes = ("seq", "exp")
-    tok_rows = normed.shape[0]
+    return lax.fori_loop(0, seq_count - 1, step, jnp.zeros_like(written)).astype(BF)
+
+
+def move(values, change):
+    exp_count = lax.axis_size("exp")
+    pairs = []
+    for s in range(lax.axis_size("seq")):
+        for e in range(exp_count):
+            to_s, to_e = change(s, e)
+            pairs.append((s * exp_count + e, to_s * exp_count + to_e))
+    return lax.ppermute(values, ("seq", "exp"), pairs)
+
+
+def over_x(values):
+    return move(values, lambda s, e: (s ^ 1, e))
+
+
+def over_y(values):
+    return move(values, lambda s, e: (s, e ^ 2))
+
+
+def over_core(values):
+    return move(values, lambda s, e: (s, e ^ 1))
+
+
+def along_z(values, by):
+    count = lax.axis_size("seq")
+    return move(values, lambda s, e: ((s + 2 * by) % count, e))
+
+
+def added(*terms):
+    total = terms[0].astype(F32)
+    for term in terms[1:]:
+        total = total + term.astype(F32)
+    return total
+
+
+def route_waves(normed, expert_ids, expert_weights, gate_up_weight, down, capacity):
+    tok_rows, width = normed.shape
+    choose = expert_ids.shape[1]
+    local_experts = gate_up_weight.shape[0]
     me = lax.axis_index("seq") * lax.axis_size("exp") + lax.axis_index("exp")
-    first = (me * gate_up_weight.shape[0]).astype(jnp.int32).reshape(1)
-    meta = jnp.concatenate([expert_ids.astype(F32).T, expert_weights.T], axis=0)
-    meta = lax.all_gather(meta, axes, axis=0, tiled=False)
-    gathered = lax.all_gather(normed, axes, axis=0, tiled=True)
-    partial_sums = experts(gathered, meta, first, gate_up_weight, down, capacity)
-    return lax.psum_scatter(partial_sums, axes, scatter_dimension=0, tiled=True).astype(F32)
+    first = (jnp.stack([me, me ^ 1]) * local_experts).astype(jnp.int32)
+    gap = jnp.zeros((tok_rows, ROUTE_STEP - choose), BF)
+    high, low = split(expert_weights)
+    tail = jnp.zeros((tok_rows, 128 - 3 * ROUTE_STEP), BF)
+    block = jnp.concatenate(
+        [normed, expert_ids.astype(BF), gap, high, gap, low, gap, tail], axis=1
+    )
+    weights = (gate_up_weight, down, over_core(gate_up_weight), over_core(down))
+    total = None
+    for wave in range(lax.axis_size("seq") // 2):
+        if wave:
+            block = along_z(block, 1)
+        one, two = (over_x, over_y) if wave % 2 == 0 else (over_y, over_x)
+        by_one = one(block)
+        by_two = two(block)
+        both = two(by_one)
+        own, sum_one, sum_two, sum_both = experts(
+            (block, by_one, by_two, both), first, weights, capacity, choose
+        )
+        passed = added(sum_one, two(sum_both)).astype(BF)
+        here = added(own, two(sum_two), one(passed))
+        if wave:
+            here = along_z(here.astype(BF), -wave).astype(F32)
+        total = here if total is None else total + here
+    return total
 
 
 def route_some(normed, expert_ids, expert_weights, gate_up_weight, down, capacity):
@@ -360,7 +456,8 @@
     experts_all = gate_up_weight.shape[0] * devices
     capacity = max(2, (tok_rows * choose * 6 + experts_all * 5 - 1) // (experts_all * 5))
     normed = rms_scale(stream, moe_gain).astype(BF)
-    route = route_all if devices * tok_rows * width * 4 <= 40 * 2**20 else route_some
+    planes = lax.axis_size("exp") == 4 and seq_count % 2 == 0 and choose <= ROUTE_STEP
+    route = route_waves if planes and experts_all <= 256 else route_some
     moe = route(normed, expert_ids, expert_weights, gate_up_weight, down, capacity)
     mixed = (stream.astype(F32) + moe).astype(BF)
     normed_mix = rms_scale(mixed, mixer_gain).astype(BF)
@@ -377,10 +474,10 @@
     rates = write_rate.T.reshape(heads, blocks, CH)
     entering, local_out, ends = mixer(projected, sums, rates)
     if heads % seq_count == 0:
-        dim = ends.shape[1]
+        dim = ends.shape[2] // 2
         each = heads // seq_count
         held = lax.all_to_all(ends, "seq", split_axis=0, concat_axis=0, tiled=True)
-        held = held.reshape(seq_count, each, dim, 2 * dim)
+        held = held.reshape(seq_count, each, dim + 16, 2 * dim)
         states = jnp.stack([carry(held[:, i]) for i in range(each)], axis=1)
         arriving = lax.all_to_all(
             states.reshape(seq_count * each, dim, dim), "seq", split_axis=0, concat_axis=0, tiled=True

time: 482 us -> 334 us (0.69)
  waiting for transfers between devices: 273 us -> 129 us
  blocking collectives: 98 us -> 34.8 us
  starting transfers between devices: 0.12 us -> 35.2 us
  Pallas kernels: 75.3 us -> 95.5 us
    reduce_scatter x1 -> x0, waiting for transfers between devices: 181 us -> none  [route_all(): lax.psum_scatter(partial_sums, axes, scatter_dimension=0, tiled=True)]
    ppermute x0 -> x32, waiting for transfers between devices: none -> 107 us  [move(): return lax.ppermute(values, ('seq', 'exp'), pairs)]
    all_gather x1 -> x0, waiting for transfers between devices: 69.4 us -> none  [route_all(): gathered = lax.all_gather(normed, axes, axis=0, tiled=True)]
    all_gather x1 -> x0, blocking collectives: 48.1 us -> none  [route_all(): meta = lax.all_gather(meta, axes, axis=0, tiled=False)]
    ppermute x0 -> x32, starting transfers between devices: none -> 35.2 us  [move(): return lax.ppermute(values, ('seq', 'exp'), pairs)]
    pallas_call x2 -> x5, Pallas kernels: 33.2 us -> 53.4 us  [the longest x4 50.5 us: experts(): pl.pallas_call(partial(moe_kernel, capacity, choose), in_specs=[pl.BlockS...]
    all_to_all x1, blocking collectives: 31.7 us -> 22.5 us  [local(): held = lax.all_to_all(ends, 'seq', split_axis=0, concat_axis=0, tiled=True)]
    all_to_all x1, blocking collectives: 18.2 us -> 12.3 us  [local(): lax.all_to_all(states.reshape(seq_count * each, dim, dim), 'seq', split_a...]
  transfers between devices with their start and end apart: 3 -> 33, of which waited for: 3 -> 11; matrix products, arithmetic and copies ran while one was open for 1% -> 3% of each run, Pallas kernels for 0% -> 15%
where the time goes in v2:
time: 334 us; the launch traced here: 333 us
  waiting for transfers between devices  129 us (39%)
  Pallas kernels  95.5 us (29%)
  starting transfers between devices  35.2 us (11%)
  blocking collectives  34.8 us (10%)
  between operations  14.5 us (4%)
  matrix products  12 us (4%)
  other arithmetic  8.64 us (3%)
    ppermute x32, waiting for transfers between devices, move(): return lax.ppermute(values, ('seq', 'exp'), pairs)  107 us
    pallas_call x4, Pallas kernels, experts(): pl.pallas_call(partial(moe_kernel, capacity, choose), in_specs=[pl.BlockS...  50.5 us
    pallas_call x1, Pallas kernels, mixer(): pl.pallas_call(mixer_kernel, grid=(heads,), in_specs=[part(0), part(1), p...  35.3 us
    ppermute x32, starting transfers between devices, move(): return lax.ppermute(values, ('seq', 'exp'), pairs)  35.2 us
    all_to_all x1, blocking collectives, local(): held = lax.all_to_all(ends, 'seq', split_axis=0, concat_axis=0, tiled=True)  22.5 us
    all_gather x1, waiting for transfers between devices, local(): lax.all_gather(normed_mix, 'exp', axis=0, tiled=True)  22 us
    all_to_all x1, blocking collectives, local(): lax.all_to_all(states.reshape(seq_count * each, dim, dim), 'seq', split_a...  12.3 us
    dot_general x1, matrix products, local(): jnp.einsum('rd,pde->pre', lax.all_gather(normed_mix, 'exp', axis=0, tiled...  12 us
  transfers between devices with their start and end apart: 33, of which 11 were waited for; matrix products, arithmetic and copies ran while one was open for 3% of the time, Pallas kernels for 15%

profile of v2, /device:TPU:0, one launch (start us, length us, event | category | flops | bytes accessed | tf_op | source)
XLA Modules:
  0.0 332.9 jit_solution(11533371271605671464)
XLA Ops:
  13.3 3.1 collective-permute-start.8
  16.3 14.9 %collective-permute-done.8.refs_1_ = bf16[128,2176]{1,0:T(8,128)(2,1)S(1)} collective-permute-done((bf16[128,2176]{1,0:T(8,128)(2,1)S(1)}, bf16[128,2176]{1,0:T(8,128)(2,1)S(1)}, u32[]{:S(2)}, u32[]{:S(2)}) %collective-permute-start.8) | collective-permute-done | bytes 557088 | tf_op jit(solution)/shard_map/ppermute | solution.py:339
  31.2 1.5 collective-permute-start.9
  32.7 1.5 collective-permute-start.10
  34.2 12.9 %collective-permute-done.16.refs_1_ = bf16[128,2176]{1,0:T(8,128)(2,1)S(1)} collective-permute-done((bf16[128,2176]{1,0:T(8,128)(2,1)S(1)}, bf16[128,2176]{1,0:T(8,128)(2,1)S(1)}, u32[]{:S(2)}, u32[]{:S(2)}) %collective-permute-start.16) | collective-permute-done | bytes 557088 | tf_op jit(solution)/shard_map/ppermute | solution.py:339
  47.1 1.3 collective-permute-start.11
  49.3 12.8 %collective-permute-done.24.refs_1_ = bf16[128,2176]{1,0:T(8,128)(2,1)S(1)} collective-permute-done((bf16[128,2176]{1,0:T(8,128)(2,1)S(1)}, bf16[128,2176]{1,0:T(8,128)(2,1)S(1)}, u32[]{:S(2)}, u32[]{:S(2)}) %collective-permute-start.24) | collective-permute-done | bytes 557088 | tf_op jit(solution)/shard_map/ppermute | solution.py:339
  63.1 1.5 collective-permute-start
  64.6 10.3 %collective-permute-done.17.refs_2_ = bf16[128,2176]{1,0:T(8,128)(2,1)S(1)} collective-permute-done((bf16[128,2176]{1,0:T(8,128)(2,1)S(1)}, bf16[128,2176]{1,0:T(8,128)(2,1)S(1)}, u32[]{:S(2)}, u32[]{:S(2)}) %collective-permute-start.17) | collective-permute-done | bytes 557088 | tf_op jit(solution)/shard_map/ppermute | solution.py:339
  79.6 12.7 %experts.5 = (bf16[128,2048]{1,0:T(8,128)(2,1)}, bf16[128,2048]{1,0:T(8,128)(2,1)}, bf16[128,2048]{1,0:T(8,128)(2,1)}, bf16[128,2048]{1,0:T(8,128)(2,1)}) custom-call(s32[2]{0:T(128)} %add_multiply_fusion.refs_0_, bf16[128,2176]{1,0:T(8,128)(2,1)} %copy-done.7, bf16[128,2176]{1,0:T(8,128)(2,1)} %collective-permute-done.9.refs_2_, ...), custom_call_target="tpu_custom_call" | custom-call | flops 4831838208 | bytes 25165824 | tf_op jit(solution)/shard_map/experts/pallas_call | solution.py:142
  92.3 1.3 collective-permute-start.1
  94.4 8.0 %collective-permute-done.19.refs_4_ = bf16[128,2176]{1,0:T(8,128)(2,1)S(1)} collective-permute-done((bf16[128,2176]{1,0:T(8,128)(2,1)S(1)}, bf16[128,2176]{1,0:T(8,128)(2,1)S(1)}, u32[]{:S(2)}, u32[]{:S(2)}) %collective-permute-start.19) | collective-permute-done | bytes 557088 | tf_op jit(solution)/shard_map/ppermute | solution.py:339
  103.7 12.6 %experts.6 = (bf16[128,2048]{1,0:T(8,128)(2,1)}, bf16[128,2048]{1,0:T(8,128)(2,1)}, bf16[128,2048]{1,0:T(8,128)(2,1)}, bf16[128,2048]{1,0:T(8,128)(2,1)}) custom-call(s32[2]{0:T(128)} %add_multiply_fusion.refs_0_, bf16[128,2176]{1,0:T(8,128)(2,1)} %copy-done.4, bf16[128,2176]{1,0:T(8,128)(2,1)} %copy-done.8, bf16[128,2176]{1,0:T(8,128)(2,1)} %copy-done.13, ...), custom_call_target="tpu_custom_call" | custom-call | flops 4831838208 | bytes 25165824 | tf_op jit(solution)/shard_map/experts/pallas_call | solution.py:142
  117.2 1.5 collective-permute-start.21
  118.7 12.6 %experts.7 = (bf16[128,2048]{1,0:T(8,128)(2,1)}, bf16[128,2048]{1,0:T(8,128)(2,1)}, bf16[128,2048]{1,0:T(8,128)(2,1)}, bf16[128,2048]{1,0:T(8,128)(2,1)}) custom-call(s32[2]{0:T(128)} %add_multiply_fusion.refs_0_, bf16[128,2176]{1,0:T(8,128)(2,1)} %copy-done.3, bf16[128,2176]{1,0:T(8,128)(2,1)} %copy-done.5, bf16[128,2176]{1,0:T(8,128)(2,1)} %copy-done.11, ...), custom_call_target="tpu_custom_call" | custom-call | flops 4831838208 | bytes 25165824 | tf_op jit(solution)/shard_map/experts/pallas_call | solution.py:142
  132.3 1.3 collective-permute-start.29
  133.6 12.6 %experts.4 = (bf16[128,2048]{1,0:T(8,128)(2,1)}, bf16[128,2048]{1,0:T(8,128)(2,1)}, bf16[128,2048]{1,0:T(8,128)(2,1)}, bf16[128,2048]{1,0:T(8,128)(2,1)}) custom-call(s32[2]{0:T(128)} %add_multiply_fusion.refs_0_, bf16[128,2176]{1,0:T(8,128)(2,1)} %copy-done.1, bf16[128,2176]{1,0:T(8,128)(2,1)} %copy-done.6, bf16[128,2176]{1,0:T(8,128)(2,1)} %copy-done.10, ...), custom_call_target="tpu_custom_call" | custom-call | flops 4831838208 | bytes 25165824 | tf_op jit(solution)/shard_map/experts/pallas_call | solution.py:142
  147.3 1.3 collective-permute-start.6
  149.7 12.7 %collective-permute-done.6 = bf16[128,2048]{1,0:T(8,128)(2,1)S(1)} collective-permute-done((bf16[128,2048]{1,0:T(8,128)(2,1)}, bf16[128,2048]{1,0:T(8,128)(2,1)S(1)}, u32[]{:S(2)}, u32[]{:S(2)}) %collective-permute-start.6) | collective-permute-done | bytes 524320 | tf_op jit(solution)/shard_map/ppermute | solution.py:339
  163.8 1.3 collective-permute-start.5
  165.1 8.5 %collective-permute-done.14 = bf16[128,2048]{1,0:T(8,128)(2,1)S(1)} collective-permute-done((bf16[128,2048]{1,0:T(8,128)(2,1)S(1)}, bf16[128,2048]{1,0:T(8,128)(2,1)S(1)}, u32[]{:S(2)}, u32[]{:S(2)}) %collective-permute-start.14) | collective-permute-done | bytes 524320 | tf_op jit(solution)/shard_map/ppermute | solution.py:339
  175.1 1.3 collective-permute-start.7
  176.4 3.8 %collective-permute-start.15 = (bf16[128,2048]{1,0:T(8,128)(2,1)S(1)}, bf16[128,2048]{1,0:T(8,128)(2,1)S(1)}, u32[]{:S(2)}, u32[]{:S(2)}) collective-permute-start(bf16[128,2048]{1,0:T(8,128)(2,1)S(1)} %add_convert_fusion.4), channel_id=1, source_target_pairs={{0,24},{1,25},{2,26},{3,27},{4,28},{5,29},{6,30},{7,31},{8,0},{9,1... | collective-permute-start | bytes 1572872 | tf_op jit(solution)/shard_map/ppermute | solution.py:339
  180.5 9.0 %collective-permute-done.30 = bf16[128,2048]{1,0:T(8,128)(2,1)S(1)} collective-permute-done((bf16[128,2048]{1,0:T(8,128)(2,1)S(1)}, bf16[128,2048]{1,0:T(8,128)(2,1)S(1)}, u32[]{:S(2)}, u32[]{:S(2)}) %collective-permute-start.30) | collective-permute-done | bytes 524320 | tf_op jit(solution)/shard_map/ppermute | solution.py:339
  190.1 18.1 %collective-permute-done.23 = bf16[128,2048]{1,0:T(8,128)(2,1)S(1)} collective-permute-done((bf16[128,2048]{1,0:T(8,128)(2,1)S(1)}, bf16[128,2048]{1,0:T(8,128)(2,1)S(1)}, u32[]{:S(2)}, u32[]{:S(2)}) %collective-permute-start.23) | collective-permute-done | bytes 524320 | tf_op jit(solution)/shard_map/ppermute | solution.py:339
  212.4 22.0 %all-gather.2.cloned.1.call-done = bf16[512,2048]{1,0:T(8,128)(2,1)} async-done(((bf16[128,2048]{1,0:T(8,128)(2,1)}), bf16[512,2048]{1,0:T(8,128)(2,1)}) %all-gather.2.cloned.1.call-update) | async-done | bytes 2097168 | tf_op jit(solution)/shard_map/all_gather | solution.py:466
  234.3 12.0 %convolution_bitcast_fusion.q_ref.k_ref.v_ref = f32[3,512,1024]{2,1,0:T(8,128)} fusion(bf16[3,2048,1024]{2,1,0:T(8,128)(2,1)} %param.17, bf16[512,2048]{1,0:T(8,128)(2,1)} %all-gather.2.cloned.1.call-done), kind=kOutput, calls=%fused_computation | convolution fusion | flops 6442450944 | bytes 20971520 | tf_op jit(solution)/shard_map/rd,pde->pre/dot_general | solution.py:464
  246.4 35.3 %mixer.1 = (f32[512,1024]{1,0:T(8,128)}, f32[512,1024]{1,0:T(8,128)}, bf16[8,144,256]{2,1,0:T(8,128)(2,1)}) custom-call(f32[3,512,1024]{2,1,0:T(8,128)} %convolution_bitcast_fusion.q_ref.k_ref.v_ref, f32[3,512,1024]{2,1,0:T(8,128)} %convolution_bitcast_fusion.q_ref.k_ref.v_ref, f32[3,512,1024]{2,1,0:T(8,128)} %convolution_bitcast_fusion.q_ref.k_ref.v_ref, ...), custom_call_target="tpu_custom_call" | custom-call | tf_op jit(solution)/shard_map/mixer/pallas_call | solution.py:255
  281.6 22.5 %all_to_all.10.ends_ref = bf16[8,144,256]{2,1,0:T(8,128)(2,1)} all-to-all(bf16[8,144,256]{2,1,0:T(8,128)(2,1)} %get-tuple-element.39), channel_id=1, replica_groups=mesh['seq'=8,'exp'=4] {'seq'}, dimensions={0} | all-to-all | bytes 1179648 | tf_op jit(solution)/shard_map/all_to_all | solution.py:479
  304.2 2.8 carry.1
  307.0 12.3 %all_to_all.11.state_ref = bf16[8,128,128]{2,1,0:T(8,128)(2,1)} all-to-all(bf16[8,128,128]{2,1,0:T(8,128)(2,1)} %carry.1), channel_id=1, replica_groups=mesh['seq'=8,'exp'=4] {'seq'}, dimensions={0} | all-to-all | bytes 524288 | tf_op jit(solution)/shard_map/all_to_all | solution.py:482
  319.2 6.8 %finish.1 = f32[512,1024]{1,0:T(8,128)} custom-call(f32[512,1024]{1,0:T(8,128)} %get-tuple-element.37.enter_ref, f32[512,1024]{1,0:T(8,128)} %get-tuple-element.38.local_ref, bf16[8,128,128]{2,1,0:T(8,128)(2,1)} %all_to_all.11.state_ref), custom_call_target="tpu_custom_call" | custom-call | tf_op jit(solution)/shard_map/finish/pallas_call | solution.py:305
  (132 shorter events, 26.3 us)
Async XLA Ops:
  7.2 227.2 %all-gather.2.cloned.1.call-start = ((), (), s32[]{:S(2)}) async-start(), calls=%async_computation.2 | async-start | bytes 2621440 | tf_op jit(solution)/shard_map/all_gather | solution.py:466
  7.2 71.6 %collective-permute-start.3 = (bf16[2,2048,1024]{2,1,0:T(8,128)(2,1)}, bf16[2,2048,1024]{2,1,0:T(8,128)(2,1)}, u32[]{:S(2)}, u32[]{:S(2)}) collective-permute-start(bf16[2,2048,1024]{2,1,0:T(8,128)(2,1)} %refs_5_.7), channel_id=1, source_target_pairs={{0,1},{1,0},{2,3},{3,2},{4,5},{5,4},{6,7},{7,6},{8,9},{9,8},{10,11... | collective-permute-start | bytes 25165832 | tf_op jit(solution)/shard_map/ppermute | solution.py:339
  7.7 69.9 %collective-permute-start.4 = (bf16[2,512,2048]{2,1,0:T(8,128)(2,1)}, bf16[2,512,2048]{2,1,0:T(8,128)(2,1)}, u32[]{:S(2)}, u32[]{:S(2)}) collective-permute-start(bf16[2,512,2048]{2,1,0:T(8,128)(2,1)} %refs_6_.7), channel_id=1, source_target_pairs={{0,1},{1,0},{2,3},{3,2},{4,5},{5,4},{6,7},{7,6},{8,9},{9,8},{10,11... | collective-permute-start | bytes 12582920 | tf_op jit(solution)/shard_map/ppermute | solution.py:339
  13.3 17.9 %collective-permute-start.8 = (bf16[128,2176]{1,0:T(8,128)(2,1)S(1)}, bf16[128,2176]{1,0:T(8,128)(2,1)S(1)}, u32[]{:S(2)}, u32[]{:S(2)}) collective-permute-start(bf16[128,2176]{1,0:T(8,128)(2,1)S(1)} %concatenate.3.refs_1_), channel_id=1, source_target_pairs={{0,8},{1,9},{2,10},{3,11},{4,12},{5,13},{6,14},{7,15},{8,16},{9,17... | collective-permute-start | bytes 1671176 | tf_op jit(solution)/shard_map/ppermute | solution.py:339
  31.2 15.9 %collective-permute-start.16 = (bf16[128,2176]{1,0:T(8,128)(2,1)S(1)}, bf16[128,2176]{1,0:T(8,128)(2,1)S(1)}, u32[]{:S(2)}, u32[]{:S(2)}) collective-permute-start(bf16[128,2176]{1,0:T(8,128)(2,1)S(1)} %collective-permute-done.8.refs_1_), channel_id=1, source_target_pairs={{0,8},{1,9},{2,10},{3,11},{4,12},{5,13},{6,14},{7,15},{8,16},{9,17... | collective-permute-start | bytes 1671176 | tf_op jit(solution)/shard_map/ppermute | solution.py:339
  31.2 15.9 %collective-permute-start.9 = (bf16[128,2176]{1,0:T(8,128)(2,1)S(1)}, bf16[128,2176]{1,0:T(8,128)(2,1)}, u32[]{:S(2)}, u32[]{:S(2)}) collective-permute-start(bf16[128,2176]{1,0:T(8,128)(2,1)S(1)} %collective-permute-done.8.refs_1_), channel_id=1, source_target_pairs={{0,2},{1,3},{2,0},{3,1},{4,6},{5,7},{6,4},{7,5},{8,10},{9,11},{10,... | collective-permute-start | bytes 1671176 | tf_op jit(solution)/shard_map/ppermute | solution.py:339
  32.7 15.7 %collective-permute-start.10 = (bf16[128,2176]{1,0:T(8,128)(2,1)S(1)}, bf16[128,2176]{1,0:T(8,128)(2,1)S(1)}, u32[]{:S(2)}, u32[]{:S(2)}) collective-permute-start(bf16[128,2176]{1,0:T(8,128)(2,1)S(1)} %collective-permute-done.8.refs_1_), channel_id=1, source_target_pairs={{0,4},{1,5},{2,6},{3,7},{4,0},{5,1},{6,2},{7,3},{8,12},{9,13},{10,... | collective-permute-start | bytes 1671176 | tf_op jit(solution)/shard_map/ppermute | solution.py:339
  47.1 15.0 %collective-permute-start.24 = (bf16[128,2176]{1,0:T(8,128)(2,1)S(1)}, bf16[128,2176]{1,0:T(8,128)(2,1)S(1)}, u32[]{:S(2)}, u32[]{:S(2)}) collective-permute-start(bf16[128,2176]{1,0:T(8,128)(2,1)S(1)} %collective-permute-done.16.refs_1_), channel_id=1, source_target_pairs={{0,8},{1,9},{2,10},{3,11},{4,12},{5,13},{6,14},{7,15},{8,16},{9,17... | collective-permute-start | bytes 1671176 | tf_op jit(solution)/shard_map/ppermute | solution.py:339
  47.1 16.0 %collective-permute-start.11 = (bf16[128,2176]{1,0:T(8,128)(2,1)}, bf16[128,2176]{1,0:T(8,128)(2,1)}, u32[]{:S(2)}, u32[]{:S(2)}) collective-permute-start(bf16[128,2176]{1,0:T(8,128)(2,1)} %collective-permute-done.9.refs_2_), channel_id=1, source_target_pairs={{0,4},{1,5},{2,6},{3,7},{4,0},{5,1},{6,2},{7,3},{8,12},{9,13},{10,... | collective-permute-start | bytes 1671176 | tf_op jit(solution)/shard_map/ppermute | solution.py:339
  48.4 26.5 %collective-permute-start.17 = (bf16[128,2176]{1,0:T(8,128)(2,1)S(1)}, bf16[128,2176]{1,0:T(8,128)(2,1)S(1)}, u32[]{:S(2)}, u32[]{:S(2)}) collective-permute-start(bf16[128,2176]{1,0:T(8,128)(2,1)S(1)} %collective-permute-done.16.refs_1_), channel_id=1, source_target_pairs={{0,4},{1,5},{2,6},{3,7},{4,0},{5,1},{6,2},{7,3},{8,12},{9,13},{10,... | collective-permute-start | bytes 1671176 | tf_op jit(solution)/shard_map/ppermute | solution.py:339
  62.1 14.1 %collective-permute-start.25 = (bf16[128,2176]{1,0:T(8,128)(2,1)S(1)}, bf16[128,2176]{1,0:T(8,128)(2,1)S(1)}, u32[]{:S(2)}, u32[]{:S(2)}) collective-permute-start(bf16[128,2176]{1,0:T(8,128)(2,1)S(1)} %collective-permute-done.24.refs_1_), channel_id=1, source_target_pairs={{0,2},{1,3},{2,0},{3,1},{4,6},{5,7},{6,4},{7,5},{8,10},{9,11},{10,... | collective-permute-start | bytes 1671176 | tf_op jit(solution)/shard_map/ppermute | solution.py:339
  63.1 29.2 %collective-permute-start = (bf16[128,2176]{1,0:T(8,128)(2,1)S(1)}, bf16[128,2176]{1,0:T(8,128)(2,1)S(1)}, u32[]{:S(2)}, u32[]{:S(2)}) collective-permute-start(bf16[128,2176]{1,0:T(8,128)(2,1)S(1)} %concatenate.3.refs_1_), channel_id=1, source_target_pairs={{0,4},{1,5},{2,6},{3,7},{4,0},{5,1},{6,2},{7,3},{8,12},{9,13},{10,... | collective-permute-start | bytes 1671176 | tf_op jit(solution)/shard_map/ppermute | solution.py:339
  74.9 18.8 %collective-permute-start.18 = (bf16[128,2176]{1,0:T(8,128)(2,1)S(1)}, bf16[128,2176]{1,0:T(8,128)(2,1)S(1)}, u32[]{:S(2)}, u32[]{:S(2)}) collective-permute-start(bf16[128,2176]{1,0:T(8,128)(2,1)S(1)} %collective-permute-done.16.refs_1_), channel_id=1, source_target_pairs={{0,2},{1,3},{2,0},{3,1},{4,6},{5,7},{6,4},{7,5},{8,10},{9,11},{10,... | collective-permute-start | bytes 1671176 | tf_op jit(solution)/shard_map/ppermute | solution.py:339
  76.2 26.2 %collective-permute-start.19 = (bf16[128,2176]{1,0:T(8,128)(2,1)S(1)}, bf16[128,2176]{1,0:T(8,128)(2,1)S(1)}, u32[]{:S(2)}, u32[]{:S(2)}) collective-permute-start(bf16[128,2176]{1,0:T(8,128)(2,1)S(1)} %collective-permute-done.17.refs_2_), channel_id=1, source_target_pairs={{0,2},{1,3},{2,0},{3,1},{4,6},{5,7},{6,4},{7,5},{8,10},{9,11},{10,... | collective-permute-start | bytes 1671176 | tf_op jit(solution)/shard_map/ppermute | solution.py:339
  77.6 38.7 %collective-permute-start.26 = (bf16[128,2176]{1,0:T(8,128)(2,1)S(1)}, bf16[128,2176]{1,0:T(8,128)(2,1)S(1)}, u32[]{:S(2)}, u32[]{:S(2)}) collective-permute-start(bf16[128,2176]{1,0:T(8,128)(2,1)S(1)} %collective-permute-done.24.refs_1_), channel_id=1, source_target_pairs={{0,4},{1,5},{2,6},{3,7},{4,0},{5,1},{6,2},{7,3},{8,12},{9,13},{10,... | collective-permute-start | bytes 1671176 | tf_op jit(solution)/shard_map/ppermute | solution.py:339
  78.8 38.3 %collective-permute-start.27 = (bf16[128,2176]{1,0:T(8,128)(2,1)S(1)}, bf16[128,2176]{1,0:T(8,128)(2,1)S(1)}, u32[]{:S(2)}, u32[]{:S(2)}) collective-permute-start(bf16[128,2176]{1,0:T(8,128)(2,1)S(1)} %collective-permute-done.25.refs_2_), channel_id=1, source_target_pairs={{0,4},{1,5},{2,6},{3,7},{4,0},{5,1},{6,2},{7,3},{8,12},{9,13},{10,... | collective-permute-start | bytes 1671176 | tf_op jit(solution)/shard_map/ppermute | solution.py:339
  92.3 39.0 %collective-permute-start.1 = (bf16[128,2176]{1,0:T(8,128)(2,1)S(1)}, bf16[128,2176]{1,0:T(8,128)(2,1)S(1)}, u32[]{:S(2)}, u32[]{:S(2)}) collective-permute-start(bf16[128,2176]{1,0:T(8,128)(2,1)S(1)} %concatenate.3.refs_1_), channel_id=1, source_target_pairs={{0,2},{1,3},{2,0},{3,1},{4,6},{5,7},{6,4},{7,5},{8,10},{9,11},{10,... | collective-permute-start | bytes 1671176 | tf_op jit(solution)/shard_map/ppermute | solution.py:339
  93.7 38.6 %collective-permute-start.2 = (bf16[128,2176]{1,0:T(8,128)(2,1)S(1)}, bf16[128,2176]{1,0:T(8,128)(2,1)S(1)}, u32[]{:S(2)}, u32[]{:S(2)}) collective-permute-start(bf16[128,2176]{1,0:T(8,128)(2,1)S(1)} %collective-permute-done.refs_2_), channel_id=1, source_target_pairs={{0,2},{1,3},{2,0},{3,1},{4,6},{5,7},{6,4},{7,5},{8,10},{9,11},{10,... | collective-permute-start | bytes 1671176 | tf_op jit(solution)/shard_map/ppermute | solution.py:339
  102.4 43.8 %collective-permute-start.13 = (bf16[128,2048]{1,0:T(8,128)(2,1)}, bf16[128,2048]{1,0:T(8,128)(2,1)S(1)}, u32[]{:S(2)}, u32[]{:S(2)}) collective-permute-start(bf16[128,2048]{1,0:T(8,128)(2,1)} %get-tuple-element.28), channel_id=1, source_target_pairs={{0,4},{1,5},{2,6},{3,7},{4,0},{5,1},{6,2},{7,3},{8,12},{9,13},{10,... | collective-permute-start | bytes 1572872 | tf_op jit(solution)/shard_map/ppermute | solution.py:339
  116.3 47.4 %collective-permute-start.12 = (bf16[128,2048]{1,0:T(8,128)(2,1)S(1)}, bf16[128,2048]{1,0:T(8,128)(2,1)S(1)}, u32[]{:S(2)}, u32[]{:S(2)}) collective-permute-start(bf16[128,2048]{1,0:T(8,128)(2,1)S(1)} %copy-done.27), channel_id=1, source_target_pairs={{0,4},{1,5},{2,6},{3,7},{4,0},{5,1},{6,2},{7,3},{8,12},{9,13},{10,... | collective-permute-start | bytes 1572872 | tf_op jit(solution)/shard_map/ppermute | solution.py:339
  117.2 30.1 %collective-permute-start.21 = (bf16[128,2048]{1,0:T(8,128)(2,1)}, bf16[128,2048]{1,0:T(8,128)(2,1)S(1)}, u32[]{:S(2)}, u32[]{:S(2)}) collective-permute-start(bf16[128,2048]{1,0:T(8,128)(2,1)} %get-tuple-element.32), channel_id=1, source_target_pairs={{0,2},{1,3},{2,0},{3,1},{4,6},{5,7},{6,4},{7,5},{8,10},{9,11},{10,... | collective-permute-start | bytes 1572872 | tf_op jit(solution)/shard_map/ppermute | solution.py:339
  131.4 43.7 %collective-permute-start.20 = (bf16[128,2048]{1,0:T(8,128)(2,1)S(1)}, bf16[128,2048]{1,0:T(8,128)(2,1)S(1)}, u32[]{:S(2)}, u32[]{:S(2)}) collective-permute-start(bf16[128,2048]{1,0:T(8,128)(2,1)S(1)} %copy-done.28), channel_id=1, source_target_pairs={{0,2},{1,3},{2,0},{3,1},{4,6},{5,7},{6,4},{7,5},{8,10},{9,11},{10,... | collective-permute-start | bytes 1572872 | tf_op jit(solution)/shard_map/ppermute | solution.py:339
  132.3 16.4 %collective-permute-start.29 = (bf16[128,2048]{1,0:T(8,128)(2,1)}, bf16[128,2048]{1,0:T(8,128)(2,1)S(1)}, u32[]{:S(2)}, u32[]{:S(2)}) collective-permute-start(bf16[128,2048]{1,0:T(8,128)(2,1)} %get-tuple-element.36), channel_id=1, source_target_pairs={{0,4},{1,5},{2,6},{3,7},{4,0},{5,1},{6,2},{7,3},{8,12},{9,13},{10,... | collective-permute-start | bytes 1572872 | tf_op jit(solution)/shard_map/ppermute | solution.py:339
  146.3 34.2 %collective-permute-start.28 = (bf16[128,2048]{1,0:T(8,128)(2,1)}, bf16[128,2048]{1,0:T(8,128)(2,1)S(1)}, u32[]{:S(2)}, u32[]{:S(2)}) collective-permute-start(bf16[128,2048]{1,0:T(8,128)(2,1)} %get-tuple-element.34), channel_id=1, source_target_pairs={{0,4},{1,5},{2,6},{3,7},{4,0},{5,1},{6,2},{7,3},{8,12},{9,13},{10,... | collective-permute-start | bytes 1572872 | tf_op jit(solution)/shard_map/ppermute | solution.py:339
  147.3 15.1 %collective-permute-start.6 = (bf16[128,2048]{1,0:T(8,128)(2,1)}, bf16[128,2048]{1,0:T(8,128)(2,1)S(1)}, u32[]{:S(2)}, u32[]{:S(2)}) collective-permute-start(bf16[128,2048]{1,0:T(8,128)(2,1)} %get-tuple-element.24), channel_id=1, source_target_pairs={{0,2},{1,3},{2,0},{3,1},{4,6},{5,7},{6,4},{7,5},{8,10},{9,11},{10,... | collective-permute-start | bytes 1572872 | tf_op jit(solution)/shard_map/ppermute | solution.py:339
  148.7 24.9 %collective-permute-start.14 = (bf16[128,2048]{1,0:T(8,128)(2,1)S(1)}, bf16[128,2048]{1,0:T(8,128)(2,1)S(1)}, u32[]{:S(2)}, u32[]{:S(2)}) collective-permute-start(bf16[128,2048]{1,0:T(8,128)(2,1)S(1)} %add_convert_fusion.5), channel_id=1, source_target_pairs={{0,2},{1,3},{2,0},{3,1},{4,6},{5,7},{6,4},{7,5},{8,10},{9,11},{10,... | collective-permute-start | bytes 1572872 | tf_op jit(solution)/shard_map/ppermute | solution.py:339
  162.4 14.0 %collective-permute-start.22 = (bf16[128,2048]{1,0:T(8,128)(2,1)S(1)}, bf16[128,2048]{1,0:T(8,128)(2,1)S(1)}, u32[]{:S(2)}, u32[]{:S(2)}) collective-permute-start(bf16[128,2048]{1,0:T(8,128)(2,1)S(1)} %add_convert_fusion.3), channel_id=1, source_target_pairs={{0,4},{1,5},{2,6},{3,7},{4,0},{5,1},{6,2},{7,3},{8,12},{9,13},{10,... | collective-permute-start | bytes 1572872 | tf_op jit(solution)/shard_map/ppermute | solution.py:339
  163.8 26.0 %collective-permute-start.5 = (bf16[128,2048]{1,0:T(8,128)(2,1)S(1)}, bf16[128,2048]{1,0:T(8,128)(2,1)S(1)}, u32[]{:S(2)}, u32[]{:S(2)}) collective-permute-start(bf16[128,2048]{1,0:T(8,128)(2,1)S(1)} %copy-done.29), channel_id=1, source_target_pairs={{0,2},{1,3},{2,0},{3,1},{4,6},{5,7},{6,4},{7,5},{8,10},{9,11},{10,... | collective-permute-start | bytes 1572872 | tf_op jit(solution)/shard_map/ppermute | solution.py:339
  173.6 15.9 %collective-permute-start.30 = (bf16[128,2048]{1,0:T(8,128)(2,1)S(1)}, bf16[128,2048]{1,0:T(8,128)(2,1)S(1)}, u32[]{:S(2)}, u32[]{:S(2)}) collective-permute-start(bf16[128,2048]{1,0:T(8,128)(2,1)S(1)} %add_convert_fusion.1), channel_id=1, source_target_pairs={{0,2},{1,3},{2,0},{3,1},{4,6},{5,7},{6,4},{7,5},{8,10},{9,11},{10,... | collective-permute-start | bytes 1572872 | tf_op jit(solution)/shard_map/ppermute | solution.py:339
  175.1 14.7 %collective-permute-start.7 = (bf16[128,2048]{1,0:T(8,128)(2,1)S(1)}, bf16[128,2048]{1,0:T(8,128)(2,1)S(1)}, u32[]{:S(2)}, u32[]{:S(2)}) collective-permute-start(bf16[128,2048]{1,0:T(8,128)(2,1)S(1)} %add_convert_fusion.6), channel_id=1, source_target_pairs={{0,4},{1,5},{2,6},{3,7},{4,0},{5,1},{6,2},{7,3},{8,12},{9,13},{10,... | collective-permute-start | bytes 1572872 | tf_op jit(solution)/shard_map/ppermute | solution.py:339
  180.5 27.7 %collective-permute-start.23 = (bf16[128,2048]{1,0:T(8,128)(2,1)S(1)}, bf16[128,2048]{1,0:T(8,128)(2,1)S(1)}, u32[]{:S(2)}, u32[]{:S(2)}) collective-permute-start(bf16[128,2048]{1,0:T(8,128)(2,1)S(1)} %add_convert_fusion.2), channel_id=1, source_target_pairs={{0,16},{1,17},{2,18},{3,19},{4,20},{5,21},{6,22},{7,23},{8,24},{9,... | collective-permute-start | bytes 1572872 | tf_op jit(solution)/shard_map/ppermute | solution.py:339
  189.8 18.4 %collective-permute-start.31 = (bf16[128,2048]{1,0:T(8,128)(2,1)S(1)}, bf16[128,2048]{1,0:T(8,128)(2,1)S(1)}, u32[]{:S(2)}, u32[]{:S(2)}) collective-permute-start(bf16[128,2048]{1,0:T(8,128)(2,1)S(1)} %add_convert_fusion), channel_id=1, source_target_pairs={{0,8},{1,9},{2,10},{3,11},{4,12},{5,13},{6,14},{7,15},{8,16},{9,17... | collective-permute-start | bytes 1572872 | tf_op jit(solution)/shard_map/ppermute | solution.py:339
  (31 other events, 751.7 us)
Sparse Core Ops, SparseCore 0:
  210.1 24.1 all-gather.1

commit v3 on v2

--- a/solution.py
+++ b/solution.py
@@ -48,8 +48,8 @@
 def moe_kernel(capacity, choose, *refs):
     first_ref, *block_refs = refs[:5]
     weight_refs = refs[5:9]
-    out_refs = refs[9:13]
-    gate_up_ref, down_ref, rows_ref, back_ref, sem = refs[13:]
+    out_refs = refs[-9:-5]
+    gate_up_ref, down_ref, rows_ref, back_ref, sem = refs[-5:]
     tok, wide = block_refs[0].shape
     width = rows_ref.shape[2]
     experts_here = gate_up_ref.shape[0]
@@ -132,7 +132,7 @@
         out_refs[2 * pair + 1][...] = summed[tok:]
 
 
-def experts(blocks, first, weights, capacity, choose):
+def experts(blocks, first, weights, after, capacity, choose):
     tok, wide = blocks[0].shape
     gate_up_weight, down = weights[:2]
     local_experts, width, double = gate_up_weight.shape
@@ -143,7 +143,7 @@
         partial(moe_kernel, capacity, choose),
         in_specs=[pl.BlockSpec(memory_space=pltpu.SMEM)]
         + [whole] * 4
-        + [pl.BlockSpec(memory_space=pl.ANY)] * 4,
+        + [pl.BlockSpec(memory_space=pl.ANY)] * (4 + len(after)),
         out_specs=[whole] * 4,
         out_shape=[jax.ShapeDtypeStruct((tok, width), BF)] * 4,
         scratch_shapes=[
@@ -160,7 +160,7 @@
             transcendentals=0,
         ),
         name="experts",
-    )(first, *blocks, *weights)
+    )(first, *blocks, *weights, *after)
 
 
 def unit_rows(values):
@@ -377,6 +377,7 @@
     )
     weights = (gate_up_weight, down, over_core(gate_up_weight), over_core(down))
     total = None
+    after = ()
     for wave in range(lax.axis_size("seq") // 2):
         if wave:
             block = along_z(block, 1)
@@ -385,8 +386,9 @@
         by_two = two(block)
         both = two(by_one)
         own, sum_one, sum_two, sum_both = experts(
-            (block, by_one, by_two, both), first, weights, capacity, choose
-        )
+            (block, by_one, by_two, both), first, weights, after, capacity, choose
+        )
+        after = (own,)
         passed = added(sum_one, two(sum_both)).astype(BF)
         here = added(own, two(sum_two), one(passed))
         if wave:

time: 334 us -> 330 us (0.988)
  waiting for transfers between devices: 129 us -> 123 us
    ppermute x32, waiting for transfers between devices: 107 us -> 101 us  [move(): return lax.ppermute(values, ('seq', 'exp'), pairs)]
  transfers between devices with their start and end apart: 33 -> 33, of which waited for: 11 -> 12; matrix products, arithmetic and copies ran while one was open for 3% -> 3% of each run, Pallas kernels for 15% -> 15%
where the time goes in v3:
time: 330 us; the launch traced here: 329 us
  waiting for transfers between devices  123 us (37%)
  Pallas kernels  95.6 us (29%)
  blocking collectives  34.8 us (11%)
  starting transfers between devices  34.1 us (10%)
  between operations  14.5 us (4%)
  matrix products  12 us (4%)
  other arithmetic  9.68 us (3%)
  local copies, waits for them, and re-layouts  5.99 us (2%)
    ppermute x32, waiting for transfers between devices, move(): return lax.ppermute(values, ('seq', 'exp'), pairs)  101 us
    pallas_call x4, Pallas kernels, experts(): pl.pallas_call(partial(moe_kernel, capacity, choose), in_specs=[pl.BlockS...  50.7 us
    pallas_call x1, Pallas kernels, mixer(): pl.pallas_call(mixer_kernel, grid=(heads,), in_specs=[part(0), part(1), p...  35.3 us
    ppermute x32, starting transfers between devices, move(): return lax.ppermute(values, ('seq', 'exp'), pairs)  34.1 us
    all_to_all x1, blocking collectives, local(): held = lax.all_to_all(ends, 'seq', split_axis=0, concat_axis=0, tiled=True)  22.5 us
    all_gather x1, waiting for transfers between devices, local(): lax.all_gather(normed_mix, 'exp', axis=0, tiled=True)  21.3 us
    all_to_all x1, blocking collectives, local(): lax.all_to_all(states.reshape(seq_count * each, dim, dim), 'seq', split_a...  12.3 us
    dot_general x1, matrix products, local(): jnp.einsum('rd,pde->pre', lax.all_gather(normed_mix, 'exp', axis=0, tiled...  12 us
  transfers between devices with their start and end apart: 33, of which 12 were waited for; matrix products, arithmetic and copies ran while one was open for 3% of the time, Pallas kernels for 15%

profile of v3, /device:TPU:0, one launch (start us, length us, event | category | flops | bytes accessed | tf_op | source)
XLA Modules:
  0.0 329.4 jit_solution(4552124418789108380)
XLA Ops:
  13.3 3.1 collective-permute-start.8
  16.3 1.5 collective-permute-start
  17.8 1.5 collective-permute-start.1
  19.3 11.9 %collective-permute-done.8.refs_1_ = bf16[128,2176]{1,0:T(8,128)(2,1)S(1)} collective-permute-done((bf16[128,2176]{1,0:T(8,128)(2,1)S(1)}, bf16[128,2176]{1,0:T(8,128)(2,1)S(1)}, u32[]{:S(2)}, u32[]{:S(2)}) %collective-permute-start.8) | collective-permute-done | bytes 557088 | tf_op jit(solution)/shard_map/ppermute | solution.py:339
  31.2 1.6 collective-permute-start.2
  33.4 13.7 %collective-permute-done.16.refs_1_ = bf16[128,2176]{1,0:T(8,128)(2,1)S(1)} collective-permute-done((bf16[128,2176]{1,0:T(8,128)(2,1)S(1)}, bf16[128,2176]{1,0:T(8,128)(2,1)S(1)}, u32[]{:S(2)}, u32[]{:S(2)}) %collective-permute-start.16) | collective-permute-done | bytes 557088 | tf_op jit(solution)/shard_map/ppermute | solution.py:339
  49.2 8.2 %collective-permute-done.9.refs_2_ = bf16[128,2176]{1,0:T(8,128)(2,1)S(1)} collective-permute-done((bf16[128,2176]{1,0:T(8,128)(2,1)S(1)}, bf16[128,2176]{1,0:T(8,128)(2,1)S(1)}, u32[]{:S(2)}, u32[]{:S(2)}) %collective-permute-start.9) | collective-permute-done | bytes 557088 | tf_op jit(solution)/shard_map/ppermute | solution.py:339
  58.6 3.4 %collective-permute-done.17.refs_2_ = bf16[128,2176]{1,0:T(8,128)(2,1)S(1)} collective-permute-done((bf16[128,2176]{1,0:T(8,128)(2,1)S(1)}, bf16[128,2176]{1,0:T(8,128)(2,1)S(1)}, u32[]{:S(2)}, u32[]{:S(2)}) %collective-permute-start.17) | collective-permute-done | bytes 557088 | tf_op jit(solution)/shard_map/ppermute | solution.py:339
  62.9 1.5 collective-permute-start.25
  65.6 1.5 collective-permute-start.19
  67.1 12.6 %experts.4 = (bf16[128,2048]{1,0:T(8,128)(2,1)}, bf16[128,2048]{1,0:T(8,128)(2,1)}, bf16[128,2048]{1,0:T(8,128)(2,1)}, bf16[128,2048]{1,0:T(8,128)(2,1)}) custom-call(s32[2]{0:T(128)} %add_multiply_fusion.refs_0_, bf16[128,2176]{1,0:T(8,128)(2,1)} %copy-done.1, bf16[128,2176]{1,0:T(8,128)(2,1)} %copy-done.11, bf16[128,2176]{1,0:T(8,128)(2,1)} %copy-done.12, ...), custom_call_target="tpu_custom_call" | custom-call | flops 4831838208 | bytes 25165824 | tf_op jit(solution)/shard_map/experts/pallas_call | solution.py:142
  80.4 1.5 collective-permute-start.27
  81.9 3.9 %collective-permute-done.11.refs_4_ = bf16[128,2176]{1,0:T(8,128)(2,1)S(1)} collective-permute-done((bf16[128,2176]{1,0:T(8,128)(2,1)S(1)}, bf16[128,2176]{1,0:T(8,128)(2,1)S(1)}, u32[]{:S(2)}, u32[]{:S(2)}) %collective-permute-start.11) | collective-permute-done | bytes 557088 | tf_op jit(solution)/shard_map/ppermute | solution.py:339
  86.6 12.6 %experts.5 = (bf16[128,2048]{1,0:T(8,128)(2,1)}, bf16[128,2048]{1,0:T(8,128)(2,1)}, bf16[128,2048]{1,0:T(8,128)(2,1)}, bf16[128,2048]{1,0:T(8,128)(2,1)}) custom-call(s32[2]{0:T(128)} %add_multiply_fusion.refs_0_, bf16[128,2176]{1,0:T(8,128)(2,1)} %copy-done.8, bf16[128,2176]{1,0:T(8,128)(2,1)} %copy-done.10, bf16[128,2176]{1,0:T(8,128)(2,1)} %copy-done.16, ...), custom_call_target="tpu_custom_call" | custom-call | flops 4831838208 | bytes 25165824 | tf_op jit(solution)/shard_map/experts/pallas_call | solution.py:142
  102.2 12.6 %experts.6 = (bf16[128,2048]{1,0:T(8,128)(2,1)}, bf16[128,2048]{1,0:T(8,128)(2,1)}, bf16[128,2048]{1,0:T(8,128)(2,1)}, bf16[128,2048]{1,0:T(8,128)(2,1)}) custom-call(s32[2]{0:T(128)} %add_multiply_fusion.refs_0_, bf16[128,2176]{1,0:T(8,128)(2,1)} %copy-done.6, bf16[128,2176]{1,0:T(8,128)(2,1)} %copy-done.9, bf16[128,2176]{1,0:T(8,128)(2,1)} %copy-done.17, ...), custom_call_target="tpu_custom_call" | custom-call | flops 4831838208 | bytes 25165824 | tf_op jit(solution)/shard_map/experts/pallas_call | solution.py:142
  117.7 12.8 %experts.7 = (bf16[128,2048]{1,0:T(8,128)(2,1)}, bf16[128,2048]{1,0:T(8,128)(2,1)}, bf16[128,2048]{1,0:T(8,128)(2,1)}, bf16[128,2048]{1,0:T(8,128)(2,1)}) custom-call(s32[2]{0:T(128)} %add_multiply_fusion.refs_0_, bf16[128,2176]{1,0:T(8,128)(2,1)} %copy-done.7, bf16[128,2176]{1,0:T(8,128)(2,1)} %copy-done.13, bf16[128,2176]{1,0:T(8,128)(2,1)} %copy-done.15, ...), custom_call_target="tpu_custom_call" | custom-call | flops 4831838208 | bytes 25165824 | tf_op jit(solution)/shard_map/experts/pallas_call | solution.py:142
  134.0 11.7 %collective-permute-done.29 = bf16[128,2048]{1,0:T(8,128)(2,1)S(1)} collective-permute-done((bf16[128,2048]{1,0:T(8,128)(2,1)}, bf16[128,2048]{1,0:T(8,128)(2,1)S(1)}, u32[]{:S(2)}, u32[]{:S(2)}) %collective-permute-start.29) | collective-permute-done | bytes 524320 | tf_op jit(solution)/shard_map/ppermute | solution.py:339
  147.9 4.5 %collective-permute-done.6 = bf16[128,2048]{1,0:T(8,128)(2,1)S(1)} collective-permute-done((bf16[128,2048]{1,0:T(8,128)(2,1)S(1)}, bf16[128,2048]{1,0:T(8,128)(2,1)S(1)}, u32[]{:S(2)}, u32[]{:S(2)}) %collective-permute-start.6) | collective-permute-done | bytes 524320 | tf_op jit(solution)/shard_map/ppermute | solution.py:339
  153.6 1.6 collective-permute-start.5
  155.2 8.5 %collective-permute-done.14 = bf16[128,2048]{1,0:T(8,128)(2,1)S(1)} collective-permute-done((bf16[128,2048]{1,0:T(8,128)(2,1)S(1)}, bf16[128,2048]{1,0:T(8,128)(2,1)S(1)}, u32[]{:S(2)}, u32[]{:S(2)}) %collective-permute-start.14) | collective-permute-done | bytes 524320 | tf_op jit(solution)/shard_map/ppermute | solution.py:339
  164.9 1.6 collective-permute-start.7
  166.5 1.7 collective-permute-done.22
  168.2 2.5 collective-permute-start.15
  171.0 10.3 %collective-permute-done.30 = bf16[128,2048]{1,0:T(8,128)(2,1)S(1)} collective-permute-done((bf16[128,2048]{1,0:T(8,128)(2,1)S(1)}, bf16[128,2048]{1,0:T(8,128)(2,1)S(1)}, u32[]{:S(2)}, u32[]{:S(2)}) %collective-permute-start.30) | collective-permute-done | bytes 524320 | tf_op jit(solution)/shard_map/ppermute | solution.py:339
  181.7 23.6 %collective-permute-done.23 = bf16[128,2048]{1,0:T(8,128)(2,1)S(1)} collective-permute-done((bf16[128,2048]{1,0:T(8,128)(2,1)S(1)}, bf16[128,2048]{1,0:T(8,128)(2,1)S(1)}, u32[]{:S(2)}, u32[]{:S(2)}) %collective-permute-start.23) | collective-permute-done | bytes 524320 | tf_op jit(solution)/shard_map/ppermute | solution.py:339
  209.5 21.3 %all-gather.2.cloned.1.call-done = bf16[512,2048]{1,0:T(8,128)(2,1)} async-done(((bf16[128,2048]{1,0:T(8,128)(2,1)}), bf16[512,2048]{1,0:T(8,128)(2,1)}) %all-gather.2.cloned.1.call-update) | async-done | bytes 2097168 | tf_op jit(solution)/shard_map/all_gather | solution.py:468
  230.8 12.0 %convolution_bitcast_fusion.q_ref.k_ref.v_ref = f32[3,512,1024]{2,1,0:T(8,128)} fusion(bf16[3,2048,1024]{2,1,0:T(8,128)(2,1)} %param.17, bf16[512,2048]{1,0:T(8,128)(2,1)} %all-gather.2.cloned.1.call-done), kind=kOutput, calls=%fused_computation | convolution fusion | flops 6442450944 | bytes 20971520 | tf_op jit(solution)/shard_map/rd,pde->pre/dot_general | solution.py:466
  242.8 35.3 %mixer.1 = (f32[512,1024]{1,0:T(8,128)}, f32[512,1024]{1,0:T(8,128)}, bf16[8,144,256]{2,1,0:T(8,128)(2,1)}) custom-call(f32[3,512,1024]{2,1,0:T(8,128)} %convolution_bitcast_fusion.q_ref.k_ref.v_ref, f32[3,512,1024]{2,1,0:T(8,128)} %convolution_bitcast_fusion.q_ref.k_ref.v_ref, f32[3,512,1024]{2,1,0:T(8,128)} %convolution_bitcast_fusion.q_ref.k_ref.v_ref, ...), custom_call_target="tpu_custom_call" | custom-call | tf_op jit(solution)/shard_map/mixer/pallas_call | solution.py:255
  278.1 22.5 %all_to_all.10.ends_ref = bf16[8,144,256]{2,1,0:T(8,128)(2,1)} all-to-all(bf16[8,144,256]{2,1,0:T(8,128)(2,1)} %get-tuple-element.39), channel_id=1, replica_groups=mesh['seq'=8,'exp'=4] {'seq'}, dimensions={0} | all-to-all | bytes 1179648 | tf_op jit(solution)/shard_map/all_to_all | solution.py:481
  300.6 2.8 carry.1
  303.5 12.3 %all_to_all.11.state_ref = bf16[8,128,128]{2,1,0:T(8,128)(2,1)} all-to-all(bf16[8,128,128]{2,1,0:T(8,128)(2,1)} %carry.1), channel_id=1, replica_groups=mesh['seq'=8,'exp'=4] {'seq'}, dimensions={0} | all-to-all | bytes 524288 | tf_op jit(solution)/shard_map/all_to_all | solution.py:484
  315.7 6.8 %finish.1 = f32[512,1024]{1,0:T(8,128)} custom-call(f32[512,1024]{1,0:T(8,128)} %get-tuple-element.37.enter_ref, f32[512,1024]{1,0:T(8,128)} %get-tuple-element.38.local_ref, bf16[8,128,128]{2,1,0:T(8,128)(2,1)} %all_to_all.11.state_ref), custom_call_target="tpu_custom_call" | custom-call | tf_op jit(solution)/shard_map/finish/pallas_call | solution.py:305
  (132 shorter events, 32.1 us)
Async XLA Ops:
  7.2 223.7 %all-gather.2.cloned.1.call-start = ((), (), s32[]{:S(2)}) async-start(), calls=%async_computation.2 | async-start | bytes 2621440 | tf_op jit(solution)/shard_map/all_gather | solution.py:468
  7.2 58.4 %collective-permute-start.3 = (bf16[2,2048,1024]{2,1,0:T(8,128)(2,1)}, bf16[2,2048,1024]{2,1,0:T(8,128)(2,1)}, u32[]{:S(2)}, u32[]{:S(2)}) collective-permute-start(bf16[2,2048,1024]{2,1,0:T(8,128)(2,1)} %refs_5_.7), channel_id=1, source_target_pairs={{0,1},{1,0},{2,3},{3,2},{4,5},{5,4},{6,7},{7,6},{8,9},{9,8},{10,11... | collective-permute-start | bytes 25165832 | tf_op jit(solution)/shard_map/ppermute | solution.py:339
  7.7 57.3 %collective-permute-start.4 = (bf16[2,512,2048]{2,1,0:T(8,128)(2,1)}, bf16[2,512,2048]{2,1,0:T(8,128)(2,1)}, u32[]{:S(2)}, u32[]{:S(2)}) collective-permute-start(bf16[2,512,2048]{2,1,0:T(8,128)(2,1)} %refs_6_.7), channel_id=1, source_target_pairs={{0,1},{1,0},{2,3},{3,2},{4,5},{5,4},{6,7},{7,6},{8,9},{9,8},{10,11... | collective-permute-start | bytes 12582920 | tf_op jit(solution)/shard_map/ppermute | solution.py:339
  13.3 17.9 %collective-permute-start.8 = (bf16[128,2176]{1,0:T(8,128)(2,1)S(1)}, bf16[128,2176]{1,0:T(8,128)(2,1)S(1)}, u32[]{:S(2)}, u32[]{:S(2)}) collective-permute-start(bf16[128,2176]{1,0:T(8,128)(2,1)S(1)} %concatenate.3.refs_1_), channel_id=1, source_target_pairs={{0,8},{1,9},{2,10},{3,11},{4,12},{5,13},{6,14},{7,15},{8,16},{9,17... | collective-permute-start | bytes 1671176 | tf_op jit(solution)/shard_map/ppermute | solution.py:339
  16.3 14.9 %collective-permute-start = (bf16[128,2176]{1,0:T(8,128)(2,1)S(1)}, bf16[128,2176]{1,0:T(8,128)(2,1)S(1)}, u32[]{:S(2)}, u32[]{:S(2)}) collective-permute-start(bf16[128,2176]{1,0:T(8,128)(2,1)S(1)} %concatenate.3.refs_1_), channel_id=1, source_target_pairs={{0,4},{1,5},{2,6},{3,7},{4,0},{5,1},{6,2},{7,3},{8,12},{9,13},{10,... | collective-permute-start | bytes 1671176 | tf_op jit(solution)/shard_map/ppermute | solution.py:339
  17.8 15.0 %collective-permute-start.1 = (bf16[128,2176]{1,0:T(8,128)(2,1)S(1)}, bf16[128,2176]{1,0:T(8,128)(2,1)S(1)}, u32[]{:S(2)}, u32[]{:S(2)}) collective-permute-start(bf16[128,2176]{1,0:T(8,128)(2,1)S(1)} %concatenate.3.refs_1_), channel_id=1, source_target_pairs={{0,2},{1,3},{2,0},{3,1},{4,6},{5,7},{6,4},{7,5},{8,10},{9,11},{10,... | collective-permute-start | bytes 1671176 | tf_op jit(solution)/shard_map/ppermute | solution.py:339
  31.2 15.9 %collective-permute-start.16 = (bf16[128,2176]{1,0:T(8,128)(2,1)S(1)}, bf16[128,2176]{1,0:T(8,128)(2,1)S(1)}, u32[]{:S(2)}, u32[]{:S(2)}) collective-permute-start(bf16[128,2176]{1,0:T(8,128)(2,1)S(1)} %collective-permute-done.8.refs_1_), channel_id=1, source_target_pairs={{0,8},{1,9},{2,10},{3,11},{4,12},{5,13},{6,14},{7,15},{8,16},{9,17... | collective-permute-start | bytes 1671176 | tf_op jit(solution)/shard_map/ppermute | solution.py:339
  31.2 17.1 %collective-permute-start.2 = (bf16[128,2176]{1,0:T(8,128)(2,1)S(1)}, bf16[128,2176]{1,0:T(8,128)(2,1)S(1)}, u32[]{:S(2)}, u32[]{:S(2)}) collective-permute-start(bf16[128,2176]{1,0:T(8,128)(2,1)S(1)} %collective-permute-done.refs_2_), channel_id=1, source_target_pairs={{0,2},{1,3},{2,0},{3,1},{4,6},{5,7},{6,4},{7,5},{8,10},{9,11},{10,... | collective-permute-start | bytes 1671176 | tf_op jit(solution)/shard_map/ppermute | solution.py:339
  32.8 24.5 %collective-permute-start.9 = (bf16[128,2176]{1,0:T(8,128)(2,1)S(1)}, bf16[128,2176]{1,0:T(8,128)(2,1)S(1)}, u32[]{:S(2)}, u32[]{:S(2)}) collective-permute-start(bf16[128,2176]{1,0:T(8,128)(2,1)S(1)} %collective-permute-done.8.refs_1_), channel_id=1, source_target_pairs={{0,2},{1,3},{2,0},{3,1},{4,6},{5,7},{6,4},{7,5},{8,10},{9,11},{10,... | collective-permute-start | bytes 1671176 | tf_op jit(solution)/shard_map/ppermute | solution.py:339
  47.1 14.8 %collective-permute-start.17 = (bf16[128,2176]{1,0:T(8,128)(2,1)S(1)}, bf16[128,2176]{1,0:T(8,128)(2,1)S(1)}, u32[]{:S(2)}, u32[]{:S(2)}) collective-permute-start(bf16[128,2176]{1,0:T(8,128)(2,1)S(1)} %collective-permute-done.16.refs_1_), channel_id=1, source_target_pairs={{0,4},{1,5},{2,6},{3,7},{4,0},{5,1},{6,2},{7,3},{8,12},{9,13},{10,... | collective-permute-start | bytes 1671176 | tf_op jit(solution)/shard_map/ppermute | solution.py:339
  48.4 14.6 %collective-permute-start.24 = (bf16[128,2176]{1,0:T(8,128)(2,1)S(1)}, bf16[128,2176]{1,0:T(8,128)(2,1)S(1)}, u32[]{:S(2)}, u32[]{:S(2)}) collective-permute-start(bf16[128,2176]{1,0:T(8,128)(2,1)S(1)} %collective-permute-done.16.refs_1_), channel_id=1, source_target_pairs={{0,8},{1,9},{2,10},{3,11},{4,12},{5,13},{6,14},{7,15},{8,16},{9,17... | collective-permute-start | bytes 1671176 | tf_op jit(solution)/shard_map/ppermute | solution.py:339
  57.3 22.5 %collective-permute-start.10 = (bf16[128,2176]{1,0:T(8,128)(2,1)S(1)}, bf16[128,2176]{1,0:T(8,128)(2,1)S(1)}, u32[]{:S(2)}, u32[]{:S(2)}) collective-permute-start(bf16[128,2176]{1,0:T(8,128)(2,1)S(1)} %collective-permute-done.8.refs_1_), channel_id=1, source_target_pairs={{0,4},{1,5},{2,6},{3,7},{4,0},{5,1},{6,2},{7,3},{8,12},{9,13},{10,... | collective-permute-start | bytes 1671176 | tf_op jit(solution)/shard_map/ppermute | solution.py:339
  61.9 23.9 %collective-permute-start.11 = (bf16[128,2176]{1,0:T(8,128)(2,1)S(1)}, bf16[128,2176]{1,0:T(8,128)(2,1)S(1)}, u32[]{:S(2)}, u32[]{:S(2)}) collective-permute-start(bf16[128,2176]{1,0:T(8,128)(2,1)S(1)} %collective-permute-done.9.refs_2_), channel_id=1, source_target_pairs={{0,4},{1,5},{2,6},{3,7},{4,0},{5,1},{6,2},{7,3},{8,12},{9,13},{10,... | collective-permute-start | bytes 1671176 | tf_op jit(solution)/shard_map/ppermute | solution.py:339
  62.9 17.5 %collective-permute-start.25 = (bf16[128,2176]{1,0:T(8,128)(2,1)S(1)}, bf16[128,2176]{1,0:T(8,128)(2,1)S(1)}, u32[]{:S(2)}, u32[]{:S(2)}) collective-permute-start(bf16[128,2176]{1,0:T(8,128)(2,1)S(1)} %collective-permute-done.24.refs_1_), channel_id=1, source_target_pairs={{0,2},{1,3},{2,0},{3,1},{4,6},{5,7},{6,4},{7,5},{8,10},{9,11},{10,... | collective-permute-start | bytes 1671176 | tf_op jit(solution)/shard_map/ppermute | solution.py:339
  65.1 35.2 %collective-permute-start.18 = (bf16[128,2176]{1,0:T(8,128)(2,1)S(1)}, bf16[128,2176]{1,0:T(8,128)(2,1)S(1)}, u32[]{:S(2)}, u32[]{:S(2)}) collective-permute-start(bf16[128,2176]{1,0:T(8,128)(2,1)S(1)} %collective-permute-done.16.refs_1_), channel_id=1, source_target_pairs={{0,2},{1,3},{2,0},{3,1},{4,6},{5,7},{6,4},{7,5},{8,10},{9,11},{10,... | collective-permute-start | bytes 1671176 | tf_op jit(solution)/shard_map/ppermute | solution.py:339
  65.6 35.8 %collective-permute-start.19 = (bf16[128,2176]{1,0:T(8,128)(2,1)S(1)}, bf16[128,2176]{1,0:T(8,128)(2,1)S(1)}, u32[]{:S(2)}, u32[]{:S(2)}) collective-permute-start(bf16[128,2176]{1,0:T(8,128)(2,1)S(1)} %collective-permute-done.17.refs_2_), channel_id=1, source_target_pairs={{0,2},{1,3},{2,0},{3,1},{4,6},{5,7},{6,4},{7,5},{8,10},{9,11},{10,... | collective-permute-start | bytes 1671176 | tf_op jit(solution)/shard_map/ppermute | solution.py:339
  79.8 36.1 %collective-permute-start.26 = (bf16[128,2176]{1,0:T(8,128)(2,1)S(1)}, bf16[128,2176]{1,0:T(8,128)(2,1)S(1)}, u32[]{:S(2)}, u32[]{:S(2)}) collective-permute-start(bf16[128,2176]{1,0:T(8,128)(2,1)S(1)} %collective-permute-done.24.refs_1_), channel_id=1, source_target_pairs={{0,4},{1,5},{2,6},{3,7},{4,0},{5,1},{6,2},{7,3},{8,12},{9,13},{10,... | collective-permute-start | bytes 1671176 | tf_op jit(solution)/shard_map/ppermute | solution.py:339
  80.4 36.5 %collective-permute-start.27 = (bf16[128,2176]{1,0:T(8,128)(2,1)S(1)}, bf16[128,2176]{1,0:T(8,128)(2,1)S(1)}, u32[]{:S(2)}, u32[]{:S(2)}) collective-permute-start(bf16[128,2176]{1,0:T(8,128)(2,1)S(1)} %collective-permute-done.25.refs_2_), channel_id=1, source_target_pairs={{0,4},{1,5},{2,6},{3,7},{4,0},{5,1},{6,2},{7,3},{8,12},{9,13},{10,... | collective-permute-start | bytes 1671176 | tf_op jit(solution)/shard_map/ppermute | solution.py:339
  99.3 32.4 %collective-permute-start.13 = (bf16[128,2048]{1,0:T(8,128)(2,1)}, bf16[128,2048]{1,0:T(8,128)(2,1)S(1)}, u32[]{:S(2)}, u32[]{:S(2)}) collective-permute-start(bf16[128,2048]{1,0:T(8,128)(2,1)} %get-tuple-element.28), channel_id=1, source_target_pairs={{0,4},{1,5},{2,6},{3,7},{4,0},{5,1},{6,2},{7,3},{8,12},{9,13},{10,... | collective-permute-start | bytes 1572872 | tf_op jit(solution)/shard_map/ppermute | solution.py:339
  100.3 53.2 %collective-permute-start.12 = (bf16[128,2048]{1,0:T(8,128)(2,1)}, bf16[128,2048]{1,0:T(8,128)(2,1)S(1)}, u32[]{:S(2)}, u32[]{:S(2)}) collective-permute-start(bf16[128,2048]{1,0:T(8,128)(2,1)} %get-tuple-element.26), channel_id=1, source_target_pairs={{0,4},{1,5},{2,6},{3,7},{4,0},{5,1},{6,2},{7,3},{8,12},{9,13},{10,... | collective-permute-start | bytes 1572872 | tf_op jit(solution)/shard_map/ppermute | solution.py:339
  114.8 18.0 %collective-permute-start.21 = (bf16[128,2048]{1,0:T(8,128)(2,1)}, bf16[128,2048]{1,0:T(8,128)(2,1)S(1)}, u32[]{:S(2)}, u32[]{:S(2)}) collective-permute-start(bf16[128,2048]{1,0:T(8,128)(2,1)} %get-tuple-element.32), channel_id=1, source_target_pairs={{0,2},{1,3},{2,0},{3,1},{4,6},{5,7},{6,4},{7,5},{8,10},{9,11},{10,... | collective-permute-start | bytes 1572872 | tf_op jit(solution)/shard_map/ppermute | solution.py:339
  115.9 49.0 %collective-permute-start.20 = (bf16[128,2048]{1,0:T(8,128)(2,1)}, bf16[128,2048]{1,0:T(8,128)(2,1)S(1)}, u32[]{:S(2)}, u32[]{:S(2)}) collective-permute-start(bf16[128,2048]{1,0:T(8,128)(2,1)} %get-tuple-element.30), channel_id=1, source_target_pairs={{0,2},{1,3},{2,0},{3,1},{4,6},{5,7},{6,4},{7,5},{8,10},{9,11},{10,... | collective-permute-start | bytes 1572872 | tf_op jit(solution)/shard_map/ppermute | solution.py:339
  130.6 15.1 %collective-permute-start.29 = (bf16[128,2048]{1,0:T(8,128)(2,1)}, bf16[128,2048]{1,0:T(8,128)(2,1)S(1)}, u32[]{:S(2)}, u32[]{:S(2)}) collective-permute-start(bf16[128,2048]{1,0:T(8,128)(2,1)} %get-tuple-element.36), channel_id=1, source_target_pairs={{0,4},{1,5},{2,6},{3,7},{4,0},{5,1},{6,2},{7,3},{8,12},{9,13},{10,... | collective-permute-start | bytes 1572872 | tf_op jit(solution)/shard_map/ppermute | solution.py:339
  131.6 39.3 %collective-permute-start.28 = (bf16[128,2048]{1,0:T(8,128)(2,1)}, bf16[128,2048]{1,0:T(8,128)(2,1)S(1)}, u32[]{:S(2)}, u32[]{:S(2)}) collective-permute-start(bf16[128,2048]{1,0:T(8,128)(2,1)} %get-tuple-element.34), channel_id=1, source_target_pairs={{0,4},{1,5},{2,6},{3,7},{4,0},{5,1},{6,2},{7,3},{8,12},{9,13},{10,... | collective-permute-start | bytes 1572872 | tf_op jit(solution)/shard_map/ppermute | solution.py:339
  132.8 19.6 %collective-permute-start.6 = (bf16[128,2048]{1,0:T(8,128)(2,1)S(1)}, bf16[128,2048]{1,0:T(8,128)(2,1)S(1)}, u32[]{:S(2)}, u32[]{:S(2)}) collective-permute-start(bf16[128,2048]{1,0:T(8,128)(2,1)S(1)} %copy-done.29), channel_id=1, source_target_pairs={{0,2},{1,3},{2,0},{3,1},{4,6},{5,7},{6,4},{7,5},{8,10},{9,11},{10,... | collective-permute-start | bytes 1572872 | tf_op jit(solution)/shard_map/ppermute | solution.py:339
  145.7 18.0 %collective-permute-start.14 = (bf16[128,2048]{1,0:T(8,128)(2,1)S(1)}, bf16[128,2048]{1,0:T(8,128)(2,1)S(1)}, u32[]{:S(2)}, u32[]{:S(2)}) collective-permute-start(bf16[128,2048]{1,0:T(8,128)(2,1)S(1)} %add_convert_fusion.5), channel_id=1, source_target_pairs={{0,2},{1,3},{2,0},{3,1},{4,6},{5,7},{6,4},{7,5},{8,10},{9,11},{10,... | collective-permute-start | bytes 1572872 | tf_op jit(solution)/shard_map/ppermute | solution.py:339
  152.4 15.7 %collective-permute-start.22 = (bf16[128,2048]{1,0:T(8,128)(2,1)S(1)}, bf16[128,2048]{1,0:T(8,128)(2,1)S(1)}, u32[]{:S(2)}, u32[]{:S(2)}) collective-permute-start(bf16[128,2048]{1,0:T(8,128)(2,1)S(1)} %add_convert_fusion.3), channel_id=1, source_target_pairs={{0,4},{1,5},{2,6},{3,7},{4,0},{5,1},{6,2},{7,3},{8,12},{9,13},{10,... | collective-permute-start | bytes 1572872 | tf_op jit(solution)/shard_map/ppermute | solution.py:339
  153.6 28.1 %collective-permute-start.5 = (bf16[128,2048]{1,0:T(8,128)(2,1)S(1)}, bf16[128,2048]{1,0:T(8,128)(2,1)S(1)}, u32[]{:S(2)}, u32[]{:S(2)}) collective-permute-start(bf16[128,2048]{1,0:T(8,128)(2,1)S(1)} %copy-done.28), channel_id=1, source_target_pairs={{0,2},{1,3},{2,0},{3,1},{4,6},{5,7},{6,4},{7,5},{8,10},{9,11},{10,... | collective-permute-start | bytes 1572872 | tf_op jit(solution)/shard_map/ppermute | solution.py:339
  163.7 17.7 %collective-permute-start.30 = (bf16[128,2048]{1,0:T(8,128)(2,1)S(1)}, bf16[128,2048]{1,0:T(8,128)(2,1)S(1)}, u32[]{:S(2)}, u32[]{:S(2)}) collective-permute-start(bf16[128,2048]{1,0:T(8,128)(2,1)S(1)} %add_convert_fusion.1), channel_id=1, source_target_pairs={{0,2},{1,3},{2,0},{3,1},{4,6},{5,7},{6,4},{7,5},{8,10},{9,11},{10,... | collective-permute-start | bytes 1572872 | tf_op jit(solution)/shard_map/ppermute | solution.py:339
  164.9 16.8 %collective-permute-start.7 = (bf16[128,2048]{1,0:T(8,128)(2,1)S(1)}, bf16[128,2048]{1,0:T(8,128)(2,1)S(1)}, u32[]{:S(2)}, u32[]{:S(2)}) collective-permute-start(bf16[128,2048]{1,0:T(8,128)(2,1)S(1)} %add_convert_fusion.6), channel_id=1, source_target_pairs={{0,4},{1,5},{2,6},{3,7},{4,0},{5,1},{6,2},{7,3},{8,12},{9,13},{10,... | collective-permute-start | bytes 1572872 | tf_op jit(solution)/shard_map/ppermute | solution.py:339
  170.9 34.4 %collective-permute-start.23 = (bf16[128,2048]{1,0:T(8,128)(2,1)S(1)}, bf16[128,2048]{1,0:T(8,128)(2,1)S(1)}, u32[]{:S(2)}, u32[]{:S(2)}) collective-permute-start(bf16[128,2048]{1,0:T(8,128)(2,1)S(1)} %add_convert_fusion.2), channel_id=1, source_target_pairs={{0,16},{1,17},{2,18},{3,19},{4,20},{5,21},{6,22},{7,23},{8,24},{9,... | collective-permute-start | bytes 1572872 | tf_op jit(solution)/shard_map/ppermute | solution.py:339
  181.6 23.7 %collective-permute-start.31 = (bf16[128,2048]{1,0:T(8,128)(2,1)S(1)}, bf16[128,2048]{1,0:T(8,128)(2,1)S(1)}, u32[]{:S(2)}, u32[]{:S(2)}) collective-permute-start(bf16[128,2048]{1,0:T(8,128)(2,1)S(1)} %add_convert_fusion), channel_id=1, source_target_pairs={{0,8},{1,9},{2,10},{3,11},{4,12},{5,13},{6,14},{7,15},{8,16},{9,17... | collective-permute-start | bytes 1572872 | tf_op jit(solution)/shard_map/ppermute | solution.py:339
  (31 other events, 747.4 us)
Sparse Core Ops, SparseCore 0:
  207.3 23.4 all-gather.1

commit v4 on v3

--- a/solution.py
+++ b/solution.py
@@ -155,8 +155,8 @@
         ],
         compiler_params=pltpu.CompilerParams(vmem_limit_bytes=VMEM_LIMIT),
         cost_estimate=pl.CostEstimate(
-            flops=2 * here * 2 * pair_rows * width * double * 3,
-            bytes_accessed=4 * (gate_up_weight.size + down.size),
+            flops=here * pair_rows * width * double // 4,
+            bytes_accessed=tok * width,
             transcendentals=0,
         ),
         name="experts",
@@ -377,20 +377,30 @@
     )
     weights = (gate_up_weight, down, over_core(gate_up_weight), over_core(down))
     total = None
-    after = ()
+    due = [(), (), (), ()]
+    diagonal = sum_below = None
     for wave in range(lax.axis_size("seq") // 2):
         if wave:
             block = along_z(block, 1)
-        one, two = (over_x, over_y) if wave % 2 == 0 else (over_y, over_x)
+        one, two = (over_x, over_y) if wave % 4 < 2 else (over_y, over_x)
         by_one = one(block)
         by_two = two(block)
-        both = two(by_one)
+        diagonal = two(by_one) if wave % 2 == 0 else along_z(diagonal, 1)
         own, sum_one, sum_two, sum_both = experts(
-            (block, by_one, by_two, both), first, weights, after, capacity, choose
-        )
-        after = (own,)
-        passed = added(sum_one, two(sum_both)).astype(BF)
-        here = added(own, two(sum_two), one(passed))
+            (block, by_one, by_two, diagonal), first, weights, due[0], capacity, choose
+        )
+        due = due[1:] + [()]
+        due[0] += (own,)
+        from_two = two(sum_two)
+        if wave % 2 == 0:
+            sum_below = along_z(sum_both, 1)
+            here = added(own, from_two, one(sum_one))
+            due[1] += (from_two, sum_below)
+        else:
+            sum_both = added(sum_both, sum_below).astype(BF)
+            passed = added(sum_one, two(sum_both)).astype(BF)
+            here = added(own, from_two, one(passed))
+            due[1] += (from_two, passed)
         if wave:
             here = along_z(here.astype(BF), -wave).astype(F32)
         total = here if total is None else total + here
@@ -458,7 +468,7 @@
     experts_all = gate_up_weight.shape[0] * devices
     capacity = max(2, (tok_rows * choose * 6 + experts_all * 5 - 1) // (experts_all * 5))
     normed = rms_scale(stream, moe_gain).astype(BF)
-    planes = lax.axis_size("exp") == 4 and seq_count % 2 == 0 and choose <= ROUTE_STEP
+    planes = lax.axis_size("exp") == 4 and seq_count % 4 == 0 and choose <= ROUTE_STEP
     route = route_waves if planes and experts_all <= 256 else route_some
     moe = route(normed, expert_ids, expert_weights, gate_up_weight, down, capacity)
     mixed = (stream.astype(F32) + moe).astype(BF)

time: 330 us -> 329 us (level)
  waiting for transfers between devices: 123 us -> 117 us
  starting transfers between devices: 34.1 us -> 38 us
    ppermute x32, waiting for transfers between devices: 101 us -> 97.5 us  [move(): return lax.ppermute(values, ('seq', 'exp'), pairs)]
    ppermute x32, starting transfers between devices: 34.1 us -> 38 us  [move(): return lax.ppermute(values, ('seq', 'exp'), pairs)]
  transfers between devices with their start and end apart: 33 -> 33, of which waited for: 12 -> 15; matrix products, arithmetic and copies ran while one was open for 3% -> 4% of each run, Pallas kernels for 15% -> 15%
where the time goes in v4:
time: 329 us; the launch traced here: 328 us
  waiting for transfers between devices  117 us (36%)
  Pallas kernels  95.6 us (29%)
  starting transfers between devices  38 us (12%)
  blocking collectives  34.8 us (11%)
  between operations  14.5 us (4%)
  other arithmetic  12.8 us (4%)
  matrix products  12 us (4%)
  local copies, waits for them, and re-layouts  3.69 us (1%)
    ppermute x32, waiting for transfers between devices, move(): return lax.ppermute(values, ('seq', 'exp'), pairs)  97.5 us
    pallas_call x4, Pallas kernels, experts(): pl.pallas_call(partial(moe_kernel, capacity, choose), in_specs=[pl.BlockS...  50.7 us
    ppermute x32, starting transfers between devices, move(): return lax.ppermute(values, ('seq', 'exp'), pairs)  38 us
    pallas_call x1, Pallas kernels, mixer(): pl.pallas_call(mixer_kernel, grid=(heads,), in_specs=[part(0), part(1), p...  35.2 us
    all_to_all x1, blocking collectives, local(): held = lax.all_to_all(ends, 'seq', split_axis=0, concat_axis=0, tiled=True)  22.5 us
    all_gather x1, waiting for transfers between devices, local(): lax.all_gather(normed_mix, 'exp', axis=0, tiled=True)  19.2 us
    all_to_all x1, blocking collectives, local(): lax.all_to_all(states.reshape(seq_count * each, dim, dim), 'seq', split_a...  12.2 us
    dot_general x1, matrix products, local(): jnp.einsum('rd,pde->pre', lax.all_gather(normed_mix, 'exp', axis=0, tiled...  12 us
  transfers between devices with their start and end apart: 33, of which 15 were waited for; matrix products, arithmetic and copies ran while one was open for 4% of the time, Pallas kernels for 15%

profile of v4, /device:TPU:0, one launch (start us, length us, event | category | flops | bytes accessed | tf_op | source)
XLA Modules:
  0.0 328.1 jit_solution(10128909811210880741)
XLA Ops:
  13.3 3.0 collective-permute-start
  19.3 9.8 %collective-permute-done.refs_2_ = bf16[128,2176]{1,0:T(8,128)(2,1)S(1)} collective-permute-done((bf16[128,2176]{1,0:T(8,128)(2,1)S(1)}, bf16[128,2176]{1,0:T(8,128)(2,1)S(1)}, u32[]{:S(2)}, u32[]{:S(2)}) %collective-permute-start) | collective-permute-done | bytes 557088 | tf_op jit(solution)/shard_map/ppermute | solution.py:339
  29.1 1.8 collective-permute-start.2
  34.0 9.8 %collective-permute-done.2.refs_4_ = bf16[128,2176]{1,0:T(8,128)(2,1)S(1)} collective-permute-done((bf16[128,2176]{1,0:T(8,128)(2,1)S(1)}, bf16[128,2176]{1,0:T(8,128)(2,1)S(1)}, u32[]{:S(2)}, u32[]{:S(2)}) %collective-permute-start.2) | collective-permute-done | bytes 557088 | tf_op jit(solution)/shard_map/ppermute | solution.py:339
  45.3 2.4 collective-permute-done.16.refs_1_
  50.0 12.6 %experts.4 = (bf16[128,2048]{1,0:T(8,128)(2,1)}, bf16[128,2048]{1,0:T(8,128)(2,1)}, bf16[128,2048]{1,0:T(8,128)(2,1)}, bf16[128,2048]{1,0:T(8,128)(2,1)}) custom-call(s32[2]{0:T(128)} %add_multiply_fusion.refs_0_, bf16[128,2176]{1,0:T(8,128)(2,1)} %copy-done.1, bf16[128,2176]{1,0:T(8,128)(2,1)} %copy-done.14, bf16[128,2176]{1,0:T(8,128)(2,1)} %copy-done.15, ...), custom_call_target="tpu_custom_call" | custom-call | flops 100663296 | bytes 262144 | tf_op jit(solution)/shard_map/experts/pallas_call | solution.py:142
  65.0 4.5 %collective-permute-done.17.refs_2_ = bf16[128,2176]{1,0:T(8,128)(2,1)S(1)} collective-permute-done((bf16[128,2176]{1,0:T(8,128)(2,1)S(1)}, bf16[128,2176]{1,0:T(8,128)(2,1)S(1)}, u32[]{:S(2)}, u32[]{:S(2)}) %collective-permute-start.17) | collective-permute-done | bytes 557088 | tf_op jit(solution)/shard_map/ppermute | solution.py:339
  71.0 12.6 %experts.5 = (bf16[128,2048]{1,0:T(8,128)(2,1)}, bf16[128,2048]{1,0:T(8,128)(2,1)}, bf16[128,2048]{1,0:T(8,128)(2,1)}, bf16[128,2048]{1,0:T(8,128)(2,1)}) custom-call(s32[2]{0:T(128)} %add_multiply_fusion.refs_0_, bf16[128,2176]{1,0:T(8,128)(2,1)} %copy-done.12, bf16[128,2176]{1,0:T(8,128)(2,1)} %copy-done.16, bf16[128,2176]{1,0:T(8,128)(2,1)} %copy-done.17, ...), custom_call_target="tpu_custom_call" | custom-call | flops 100663296 | bytes 262144 | tf_op jit(solution)/shard_map/experts/pallas_call | solution.py:142
  85.9 2.4 collective-permute-done.23.refs_1_
  91.4 12.7 %experts.6 = (bf16[128,2048]{1,0:T(8,128)(2,1)}, bf16[128,2048]{1,0:T(8,128)(2,1)}, bf16[128,2048]{1,0:T(8,128)(2,1)}, bf16[128,2048]{1,0:T(8,128)(2,1)}) custom-call(s32[2]{0:T(128)} %add_multiply_fusion.refs_0_, bf16[128,2176]{1,0:T(8,128)(2,1)} %copy-done.19, bf16[128,2176]{1,0:T(8,128)(2,1)} %copy-done.21, bf16[128,2176]{1,0:T(8,128)(2,1)} %copy-done.23, ...), custom_call_target="tpu_custom_call" | custom-call | flops 100663296 | bytes 262144 | tf_op jit(solution)/shard_map/experts/pallas_call | solution.py:142
  104.1 2.2 collective-permute-start.28
  107.3 4.6 %collective-permute-done.24.refs_2_ = bf16[128,2176]{1,0:T(8,128)(2,1)S(1)} collective-permute-done((bf16[128,2176]{1,0:T(8,128)(2,1)S(1)}, bf16[128,2176]{1,0:T(8,128)(2,1)S(1)}, u32[]{:S(2)}, u32[]{:S(2)}) %collective-permute-start.24) | collective-permute-done | bytes 557088 | tf_op jit(solution)/shard_map/ppermute | solution.py:339
  111.9 7.9 %collective-permute-done.11.refs_9_ = bf16[128,2048]{1,0:T(8,128)(2,1)S(1)} collective-permute-done((bf16[128,2048]{1,0:T(8,128)(2,1)}, bf16[128,2048]{1,0:T(8,128)(2,1)S(1)}, u32[]{:S(2)}, u32[]{:S(2)}) %collective-permute-start.11) | collective-permute-done | bytes 524320 | tf_op jit(solution)/shard_map/ppermute | solution.py:339
  120.7 12.8 %experts.7 = (bf16[128,2048]{1,0:T(8,128)(2,1)}, bf16[128,2048]{1,0:T(8,128)(2,1)}, bf16[128,2048]{1,0:T(8,128)(2,1)}, bf16[128,2048]{1,0:T(8,128)(2,1)}) custom-call(s32[2]{0:T(128)} %add_multiply_fusion.refs_0_, bf16[128,2176]{1,0:T(8,128)(2,1)} %copy-done.20, bf16[128,2176]{1,0:T(8,128)(2,1)} %copy-done.24, bf16[128,2176]{1,0:T(8,128)(2,1)} %copy-done.25, ...), custom_call_target="tpu_custom_call" | custom-call | flops 100663296 | bytes 262144 | tf_op jit(solution)/shard_map/experts/pallas_call | solution.py:142
  134.9 1.8 collective-permute-start.29
  138.0 1.7 collective-permute-start.6
  140.0 9.8 %collective-permute-done.29 = bf16[128,2048]{1,0:T(8,128)(2,1)S(1)} collective-permute-done((bf16[128,2048]{1,0:T(8,128)(2,1)S(1)}, bf16[128,2048]{1,0:T(8,128)(2,1)S(1)}, u32[]{:S(2)}, u32[]{:S(2)}) %collective-permute-start.29) | collective-permute-done | bytes 524320 | tf_op jit(solution)/shard_map/ppermute | solution.py:339
  152.7 8.4 %collective-permute-done.20 = bf16[128,2048]{1,0:T(8,128)(2,1)S(1)} collective-permute-done((bf16[128,2048]{1,0:T(8,128)(2,1)S(1)}, bf16[128,2048]{1,0:T(8,128)(2,1)S(1)}, u32[]{:S(2)}, u32[]{:S(2)}) %collective-permute-start.20) | collective-permute-done | bytes 524320 | tf_op jit(solution)/shard_map/ppermute | solution.py:339
  162.3 2.7 collective-permute-start.22
  164.9 18.5 %collective-permute-done.14 = bf16[128,2048]{1,0:T(8,128)(2,1)S(1)} collective-permute-done((bf16[128,2048]{1,0:T(8,128)(2,1)S(1)}, bf16[128,2048]{1,0:T(8,128)(2,1)S(1)}, u32[]{:S(2)}, u32[]{:S(2)}) %collective-permute-start.14) | collective-permute-done | bytes 524320 | tf_op jit(solution)/shard_map/ppermute | solution.py:339
  183.8 2.7 collective-permute-start.15
  186.5 4.1 %collective-permute-done.27 = bf16[128,2048]{1,0:T(8,128)(2,1)S(1)} collective-permute-done((bf16[128,2048]{1,0:T(8,128)(2,1)}, bf16[128,2048]{1,0:T(8,128)(2,1)S(1)}, u32[]{:S(2)}, u32[]{:S(2)}) %collective-permute-start.27) | collective-permute-done | bytes 524320 | tf_op jit(solution)/shard_map/ppermute | solution.py:339
  190.8 1.8 collective-permute-start.31
  192.6 5.2 %collective-permute-done.15 = bf16[128,2048]{1,0:T(8,128)(2,1)S(1)} collective-permute-done((bf16[128,2048]{1,0:T(8,128)(2,1)S(1)}, bf16[128,2048]{1,0:T(8,128)(2,1)S(1)}, u32[]{:S(2)}, u32[]{:S(2)}) %collective-permute-start.15) | collective-permute-done | bytes 524320 | tf_op jit(solution)/shard_map/ppermute | solution.py:339
  197.8 8.4 %collective-permute-done.31 = bf16[128,2048]{1,0:T(8,128)(2,1)S(1)} collective-permute-done((bf16[128,2048]{1,0:T(8,128)(2,1)S(1)}, bf16[128,2048]{1,0:T(8,128)(2,1)S(1)}, u32[]{:S(2)}, u32[]{:S(2)}) %collective-permute-start.31) | collective-permute-done | bytes 524320 | tf_op jit(solution)/shard_map/ppermute | solution.py:339
  210.3 19.2 %all-gather.2.cloned.1.call-done = bf16[512,2048]{1,0:T(8,128)(2,1)} async-done(((bf16[128,2048]{1,0:T(8,128)(2,1)}), bf16[512,2048]{1,0:T(8,128)(2,1)}) %all-gather.2.cloned.1.call-update) | async-done | bytes 2097168 | tf_op jit(solution)/shard_map/all_gather | solution.py:478
  229.5 12.0 %convolution_bitcast_fusion.q_ref.k_ref.v_ref = f32[3,512,1024]{2,1,0:T(8,128)} fusion(bf16[3,2048,1024]{2,1,0:T(8,128)(2,1)} %param.17, bf16[512,2048]{1,0:T(8,128)(2,1)} %all-gather.2.cloned.1.call-done), kind=kOutput, calls=%fused_computation | convolution fusion | flops 6442450944 | bytes 20971520 | tf_op jit(solution)/shard_map/rd,pde->pre/dot_general | solution.py:476
  241.5 35.2 %mixer.1 = (f32[512,1024]{1,0:T(8,128)}, f32[512,1024]{1,0:T(8,128)}, bf16[8,144,256]{2,1,0:T(8,128)(2,1)}) custom-call(f32[3,512,1024]{2,1,0:T(8,128)} %convolution_bitcast_fusion.q_ref.k_ref.v_ref, f32[3,512,1024]{2,1,0:T(8,128)} %convolution_bitcast_fusion.q_ref.k_ref.v_ref, f32[3,512,1024]{2,1,0:T(8,128)} %convolution_bitcast_fusion.q_ref.k_ref.v_ref, ...), custom_call_target="tpu_custom_call" | custom-call | tf_op jit(solution)/shard_map/mixer/pallas_call | solution.py:255
  276.8 22.5 %all_to_all.10.ends_ref = bf16[8,144,256]{2,1,0:T(8,128)(2,1)} all-to-all(bf16[8,144,256]{2,1,0:T(8,128)(2,1)} %get-tuple-element.39), channel_id=1, replica_groups=mesh['seq'=8,'exp'=4] {'seq'}, dimensions={0} | all-to-all | bytes 1179648 | tf_op jit(solution)/shard_map/all_to_all | solution.py:491
  299.3 2.8 carry.1
  302.1 12.2 %all_to_all.11.state_ref = bf16[8,128,128]{2,1,0:T(8,128)(2,1)} all-to-all(bf16[8,128,128]{2,1,0:T(8,128)(2,1)} %carry.1), channel_id=1, replica_groups=mesh['seq'=8,'exp'=4] {'seq'}, dimensions={0} | all-to-all | bytes 524288 | tf_op jit(solution)/shard_map/all_to_all | solution.py:494
  314.4 6.8 %finish.1 = f32[512,1024]{1,0:T(8,128)} custom-call(f32[512,1024]{1,0:T(8,128)} %get-tuple-element.37.enter_ref, f32[512,1024]{1,0:T(8,128)} %get-tuple-element.38.local_ref, bf16[8,128,128]{2,1,0:T(8,128)(2,1)} %all_to_all.11.state_ref), custom_call_target="tpu_custom_call" | custom-call | tf_op jit(solution)/shard_map/finish/pallas_call | solution.py:305
  (142 shorter events, 38.5 us)
Async XLA Ops:
  7.2 222.4 %all-gather.2.cloned.1.call-start = ((), (), s32[]{:S(2)}) async-start(), calls=%async_computation.2 | async-start | bytes 2621440 | tf_op jit(solution)/shard_map/all_gather | solution.py:478
  7.2 42.8 %collective-permute-start.3 = (bf16[2,2048,1024]{2,1,0:T(8,128)(2,1)}, bf16[2,2048,1024]{2,1,0:T(8,128)(2,1)}, u32[]{:S(2)}, u32[]{:S(2)}) collective-permute-start(bf16[2,2048,1024]{2,1,0:T(8,128)(2,1)} %refs_5_.7), channel_id=1, source_target_pairs={{0,1},{1,0},{2,3},{3,2},{4,5},{5,4},{6,7},{7,6},{8,9},{9,8},{10,11... | collective-permute-start | bytes 25165832 | tf_op jit(solution)/shard_map/ppermute | solution.py:339
  7.7 40.0 %collective-permute-start.4 = (bf16[2,512,2048]{2,1,0:T(8,128)(2,1)}, bf16[2,512,2048]{2,1,0:T(8,128)(2,1)}, u32[]{:S(2)}, u32[]{:S(2)}) collective-permute-start(bf16[2,512,2048]{2,1,0:T(8,128)(2,1)} %refs_6_.7), channel_id=1, source_target_pairs={{0,1},{1,0},{2,3},{3,2},{4,5},{5,4},{6,7},{7,6},{8,9},{9,8},{10,11... | collective-permute-start | bytes 12582920 | tf_op jit(solution)/shard_map/ppermute | solution.py:339
  13.3 15.9 %collective-permute-start = (bf16[128,2176]{1,0:T(8,128)(2,1)S(1)}, bf16[128,2176]{1,0:T(8,128)(2,1)S(1)}, u32[]{:S(2)}, u32[]{:S(2)}) collective-permute-start(bf16[128,2176]{1,0:T(8,128)(2,1)S(1)} %concatenate.3.refs_1_), channel_id=1, source_target_pairs={{0,4},{1,5},{2,6},{3,7},{4,0},{5,1},{6,2},{7,3},{8,12},{9,13},{10,... | collective-permute-start | bytes 1671176 | tf_op jit(solution)/shard_map/ppermute | solution.py:339
  16.2 16.2 %collective-permute-start.7 = (bf16[128,2176]{1,0:T(8,128)(2,1)S(1)}, bf16[128,2176]{1,0:T(8,128)(2,1)S(1)}, u32[]{:S(2)}, u32[]{:S(2)}) collective-permute-start(bf16[128,2176]{1,0:T(8,128)(2,1)S(1)} %concatenate.3.refs_1_), channel_id=1, source_target_pairs={{0,8},{1,9},{2,10},{3,11},{4,12},{5,13},{6,14},{7,15},{8,16},{9,17... | collective-permute-start | bytes 1671176 | tf_op jit(solution)/shard_map/ppermute | solution.py:339
  17.8 14.7 %collective-permute-start.1 = (bf16[128,2176]{1,0:T(8,128)(2,1)S(1)}, bf16[128,2176]{1,0:T(8,128)(2,1)S(1)}, u32[]{:S(2)}, u32[]{:S(2)}) collective-permute-start(bf16[128,2176]{1,0:T(8,128)(2,1)S(1)} %concatenate.3.refs_1_), channel_id=1, source_target_pairs={{0,2},{1,3},{2,0},{3,1},{4,6},{5,7},{6,4},{7,5},{8,10},{9,11},{10,... | collective-permute-start | bytes 1671176 | tf_op jit(solution)/shard_map/ppermute | solution.py:339
  29.1 14.7 %collective-permute-start.2 = (bf16[128,2176]{1,0:T(8,128)(2,1)S(1)}, bf16[128,2176]{1,0:T(8,128)(2,1)S(1)}, u32[]{:S(2)}, u32[]{:S(2)}) collective-permute-start(bf16[128,2176]{1,0:T(8,128)(2,1)S(1)} %collective-permute-done.refs_2_), channel_id=1, source_target_pairs={{0,2},{1,3},{2,0},{3,1},{4,6},{5,7},{6,4},{7,5},{8,10},{9,11},{10,... | collective-permute-start | bytes 1671176 | tf_op jit(solution)/shard_map/ppermute | solution.py:339
  32.4 15.3 %collective-permute-start.16 = (bf16[128,2176]{1,0:T(8,128)(2,1)S(1)}, bf16[128,2176]{1,0:T(8,128)(2,1)S(1)}, u32[]{:S(2)}, u32[]{:S(2)}) collective-permute-start(bf16[128,2176]{1,0:T(8,128)(2,1)S(1)} %collective-permute-done.7.refs_1_), channel_id=1, source_target_pairs={{0,8},{1,9},{2,10},{3,11},{4,12},{5,13},{6,14},{7,15},{8,16},{9,17... | collective-permute-start | bytes 1671176 | tf_op jit(solution)/shard_map/ppermute | solution.py:339
  32.5 30.2 %collective-permute-start.8 = (bf16[128,2176]{1,0:T(8,128)(2,1)S(1)}, bf16[128,2176]{1,0:T(8,128)(2,1)S(1)}, u32[]{:S(2)}, u32[]{:S(2)}) collective-permute-start(bf16[128,2176]{1,0:T(8,128)(2,1)S(1)} %collective-permute-done.7.refs_1_), channel_id=1, source_target_pairs={{0,4},{1,5},{2,6},{3,7},{4,0},{5,1},{6,2},{7,3},{8,12},{9,13},{10,... | collective-permute-start | bytes 1671176 | tf_op jit(solution)/shard_map/ppermute | solution.py:339
  43.8 19.5 %collective-permute-start.9 = (bf16[128,2176]{1,0:T(8,128)(2,1)S(1)}, bf16[128,2176]{1,0:T(8,128)(2,1)S(1)}, u32[]{:S(2)}, u32[]{:S(2)}) collective-permute-start(bf16[128,2176]{1,0:T(8,128)(2,1)S(1)} %collective-permute-done.7.refs_1_), channel_id=1, source_target_pairs={{0,2},{1,3},{2,0},{3,1},{4,6},{5,7},{6,4},{7,5},{8,10},{9,11},{10,... | collective-permute-start | bytes 1671176 | tf_op jit(solution)/shard_map/ppermute | solution.py:339
  47.8 21.8 %collective-permute-start.10 = (bf16[128,2176]{1,0:T(8,128)(2,1)S(1)}, bf16[128,2176]{1,0:T(8,128)(2,1)S(1)}, u32[]{:S(2)}, u32[]{:S(2)}) collective-permute-start(bf16[128,2176]{1,0:T(8,128)(2,1)S(1)} %collective-permute-done.2.refs_4_), channel_id=1, source_target_pairs={{0,8},{1,9},{2,10},{3,11},{4,12},{5,13},{6,14},{7,15},{8,16},{9,17... | collective-permute-start | bytes 1671176 | tf_op jit(solution)/shard_map/ppermute | solution.py:339
  47.8 21.8 %collective-permute-start.17 = (bf16[128,2176]{1,0:T(8,128)(2,1)S(1)}, bf16[128,2176]{1,0:T(8,128)(2,1)S(1)}, u32[]{:S(2)}, u32[]{:S(2)}) collective-permute-start(bf16[128,2176]{1,0:T(8,128)(2,1)S(1)} %collective-permute-done.16.refs_1_), channel_id=1, source_target_pairs={{0,2},{1,3},{2,0},{3,1},{4,6},{5,7},{6,4},{7,5},{8,10},{9,11},{10,... | collective-permute-start | bytes 1671176 | tf_op jit(solution)/shard_map/ppermute | solution.py:339
  62.6 21.0 %collective-permute-start.12 = (bf16[128,2048]{1,0:T(8,128)(2,1)}, bf16[128,2048]{1,0:T(8,128)(2,1)S(1)}, u32[]{:S(2)}, u32[]{:S(2)}) collective-permute-start(bf16[128,2048]{1,0:T(8,128)(2,1)} %get-tuple-element.28), channel_id=1, source_target_pairs={{0,8},{1,9},{2,10},{3,11},{4,12},{5,13},{6,14},{7,15},{8,16},{9,17... | collective-permute-start | bytes 1572872 | tf_op jit(solution)/shard_map/ppermute | solution.py:339
  62.7 26.0 %collective-permute-start.18 = (bf16[128,2176]{1,0:T(8,128)(2,1)S(1)}, bf16[128,2176]{1,0:T(8,128)(2,1)S(1)}, u32[]{:S(2)}, u32[]{:S(2)}) collective-permute-start(bf16[128,2176]{1,0:T(8,128)(2,1)S(1)} %collective-permute-done.16.refs_1_), channel_id=1, source_target_pairs={{0,4},{1,5},{2,6},{3,7},{4,0},{5,1},{6,2},{7,3},{8,12},{9,13},{10,... | collective-permute-start | bytes 1671176 | tf_op jit(solution)/shard_map/ppermute | solution.py:339
  63.3 24.9 %collective-permute-start.23 = (bf16[128,2176]{1,0:T(8,128)(2,1)S(1)}, bf16[128,2176]{1,0:T(8,128)(2,1)S(1)}, u32[]{:S(2)}, u32[]{:S(2)}) collective-permute-start(bf16[128,2176]{1,0:T(8,128)(2,1)S(1)} %collective-permute-done.16.refs_1_), channel_id=1, source_target_pairs={{0,8},{1,9},{2,10},{3,11},{4,12},{5,13},{6,14},{7,15},{8,16},{9,17... | collective-permute-start | bytes 1671176 | tf_op jit(solution)/shard_map/ppermute | solution.py:339
  69.5 20.3 %collective-permute-start.19 = (bf16[128,2176]{1,0:T(8,128)(2,1)S(1)}, bf16[128,2176]{1,0:T(8,128)(2,1)S(1)}, u32[]{:S(2)}, u32[]{:S(2)}) collective-permute-start(bf16[128,2176]{1,0:T(8,128)(2,1)S(1)} %collective-permute-done.17.refs_2_), channel_id=1, source_target_pairs={{0,4},{1,5},{2,6},{3,7},{4,0},{5,1},{6,2},{7,3},{8,12},{9,13},{10,... | collective-permute-start | bytes 1671176 | tf_op jit(solution)/shard_map/ppermute | solution.py:339
  69.6 21.0 %collective-permute-start.5 = (bf16[128,2048]{1,0:T(8,128)(2,1)}, bf16[128,2048]{1,0:T(8,128)(2,1)S(1)}, u32[]{:S(2)}, u32[]{:S(2)}) collective-permute-start(bf16[128,2048]{1,0:T(8,128)(2,1)} %get-tuple-element.22), channel_id=1, source_target_pairs={{0,2},{1,3},{2,0},{3,1},{4,6},{5,7},{6,4},{7,5},{8,10},{9,11},{10,... | collective-permute-start | bytes 1572872 | tf_op jit(solution)/shard_map/ppermute | solution.py:339
  85.0 19.1 %collective-permute-start.13 = (bf16[128,2048]{1,0:T(8,128)(2,1)S(1)}, bf16[128,2048]{1,0:T(8,128)(2,1)S(1)}, u32[]{:S(2)}, u32[]{:S(2)}) collective-permute-start(bf16[128,2048]{1,0:T(8,128)(2,1)S(1)} %add_convert_fusion.6), channel_id=1, source_target_pairs={{0,2},{1,3},{2,0},{3,1},{4,6},{5,7},{6,4},{7,5},{8,10},{9,11},{10,... | collective-permute-start | bytes 1572872 | tf_op jit(solution)/shard_map/ppermute | solution.py:339
  88.3 23.6 %collective-permute-start.24 = (bf16[128,2176]{1,0:T(8,128)(2,1)S(1)}, bf16[128,2176]{1,0:T(8,128)(2,1)S(1)}, u32[]{:S(2)}, u32[]{:S(2)}) collective-permute-start(bf16[128,2176]{1,0:T(8,128)(2,1)S(1)} %collective-permute-done.23.refs_1_), channel_id=1, source_target_pairs={{0,2},{1,3},{2,0},{3,1},{4,6},{5,7},{6,4},{7,5},{8,10},{9,11},{10,... | collective-permute-start | bytes 1671176 | tf_op jit(solution)/shard_map/ppermute | solution.py:339
  88.8 23.1 %collective-permute-start.25 = (bf16[128,2176]{1,0:T(8,128)(2,1)S(1)}, bf16[128,2176]{1,0:T(8,128)(2,1)S(1)}, u32[]{:S(2)}, u32[]{:S(2)}) collective-permute-start(bf16[128,2176]{1,0:T(8,128)(2,1)S(1)} %collective-permute-done.23.refs_1_), channel_id=1, source_target_pairs={{0,4},{1,5},{2,6},{3,7},{4,0},{5,1},{6,2},{7,3},{8,12},{9,13},{10,... | collective-permute-start | bytes 1671176 | tf_op jit(solution)/shard_map/ppermute | solution.py:339
  89.8 22.0 %collective-permute-start.26 = (bf16[128,2176]{1,0:T(8,128)(2,1)S(1)}, bf16[128,2176]{1,0:T(8,128)(2,1)S(1)}, u32[]{:S(2)}, u32[]{:S(2)}) collective-permute-start(bf16[128,2176]{1,0:T(8,128)(2,1)S(1)} %collective-permute-done.19.refs_4_), channel_id=1, source_target_pairs={{0,8},{1,9},{2,10},{3,11},{4,12},{5,13},{6,14},{7,15},{8,16},{9,17... | collective-permute-start | bytes 1671176 | tf_op jit(solution)/shard_map/ppermute | solution.py:339
  90.6 29.3 %collective-permute-start.11 = (bf16[128,2048]{1,0:T(8,128)(2,1)}, bf16[128,2048]{1,0:T(8,128)(2,1)S(1)}, u32[]{:S(2)}, u32[]{:S(2)}) collective-permute-start(bf16[128,2048]{1,0:T(8,128)(2,1)} %get-tuple-element.25), channel_id=1, source_target_pairs={{0,2},{1,3},{2,0},{3,1},{4,6},{5,7},{6,4},{7,5},{8,10},{9,11},{10,... | collective-permute-start | bytes 1572872 | tf_op jit(solution)/shard_map/ppermute | solution.py:339
  104.1 29.4 %collective-permute-start.28 = (bf16[128,2048]{1,0:T(8,128)(2,1)}, bf16[128,2048]{1,0:T(8,128)(2,1)S(1)}, u32[]{:S(2)}, u32[]{:S(2)}) collective-permute-start(bf16[128,2048]{1,0:T(8,128)(2,1)} %get-tuple-element.36), channel_id=1, source_target_pairs={{0,8},{1,9},{2,10},{3,11},{4,12},{5,13},{6,14},{7,15},{8,16},{9,17... | collective-permute-start | bytes 1572872 | tf_op jit(solution)/shard_map/ppermute | solution.py:339
  134.9 14.9 %collective-permute-start.29 = (bf16[128,2048]{1,0:T(8,128)(2,1)S(1)}, bf16[128,2048]{1,0:T(8,128)(2,1)S(1)}, u32[]{:S(2)}, u32[]{:S(2)}) collective-permute-start(bf16[128,2048]{1,0:T(8,128)(2,1)S(1)} %add_convert_fusion.2), channel_id=1, source_target_pairs={{0,4},{1,5},{2,6},{3,7},{4,0},{5,1},{6,2},{7,3},{8,12},{9,13},{10,... | collective-permute-start | bytes 1572872 | tf_op jit(solution)/shard_map/ppermute | solution.py:339
  136.6 24.4 %collective-permute-start.20 = (bf16[128,2048]{1,0:T(8,128)(2,1)S(1)}, bf16[128,2048]{1,0:T(8,128)(2,1)S(1)}, u32[]{:S(2)}, u32[]{:S(2)}) collective-permute-start(bf16[128,2048]{1,0:T(8,128)(2,1)S(1)} %copy-done.34), channel_id=1, source_target_pairs={{0,4},{1,5},{2,6},{3,7},{4,0},{5,1},{6,2},{7,3},{8,12},{9,13},{10,... | collective-permute-start | bytes 1572872 | tf_op jit(solution)/shard_map/ppermute | solution.py:339
  137.0 25.1 %collective-permute-start.21 = (bf16[128,2048]{1,0:T(8,128)(2,1)S(1)}, bf16[128,2048]{1,0:T(8,128)(2,1)S(1)}, u32[]{:S(2)}, u32[]{:S(2)}) collective-permute-start(bf16[128,2048]{1,0:T(8,128)(2,1)S(1)} %copy-done.33), channel_id=1, source_target_pairs={{0,2},{1,3},{2,0},{3,1},{4,6},{5,7},{6,4},{7,5},{8,10},{9,11},{10,... | collective-permute-start | bytes 1572872 | tf_op jit(solution)/shard_map/ppermute | solution.py:339
  138.0 54.6 %collective-permute-start.6 = (bf16[128,2048]{1,0:T(8,128)(2,1)S(1)}, bf16[128,2048]{1,0:T(8,128)(2,1)S(1)}, u32[]{:S(2)}, u32[]{:S(2)}) collective-permute-start(bf16[128,2048]{1,0:T(8,128)(2,1)S(1)} %copy-done.32), channel_id=1, source_target_pairs={{0,4},{1,5},{2,6},{3,7},{4,0},{5,1},{6,2},{7,3},{8,12},{9,13},{10,... | collective-permute-start | bytes 1572872 | tf_op jit(solution)/shard_map/ppermute | solution.py:339
  139.7 43.8 %collective-permute-start.14 = (bf16[128,2048]{1,0:T(8,128)(2,1)S(1)}, bf16[128,2048]{1,0:T(8,128)(2,1)S(1)}, u32[]{:S(2)}, u32[]{:S(2)}) collective-permute-start(bf16[128,2048]{1,0:T(8,128)(2,1)S(1)} %copy-done.4), channel_id=1, source_target_pairs={{0,4},{1,5},{2,6},{3,7},{4,0},{5,1},{6,2},{7,3},{8,12},{9,13},{10,... | collective-permute-start | bytes 1572872 | tf_op jit(solution)/shard_map/ppermute | solution.py:339
  149.8 40.8 %collective-permute-start.27 = (bf16[128,2048]{1,0:T(8,128)(2,1)}, bf16[128,2048]{1,0:T(8,128)(2,1)S(1)}, u32[]{:S(2)}, u32[]{:S(2)}) collective-permute-start(bf16[128,2048]{1,0:T(8,128)(2,1)} %get-tuple-element.33), channel_id=1, source_target_pairs={{0,4},{1,5},{2,6},{3,7},{4,0},{5,1},{6,2},{7,3},{8,12},{9,13},{10,... | collective-permute-start | bytes 1572872 | tf_op jit(solution)/shard_map/ppermute | solution.py:339
  161.0 29.5 %collective-permute-start.30 = (bf16[128,2048]{1,0:T(8,128)(2,1)S(1)}, bf16[128,2048]{1,0:T(8,128)(2,1)S(1)}, u32[]{:S(2)}, u32[]{:S(2)}) collective-permute-start(bf16[128,2048]{1,0:T(8,128)(2,1)S(1)} %add_convert_fusion.1), channel_id=1, source_target_pairs={{0,2},{1,3},{2,0},{3,1},{4,6},{5,7},{6,4},{7,5},{8,10},{9,11},{10,... | collective-permute-start | bytes 1572872 | tf_op jit(solution)/shard_map/ppermute | solution.py:339
  162.3 30.3 %collective-permute-start.22 = (bf16[128,2048]{1,0:T(8,128)(2,1)S(1)}, bf16[128,2048]{1,0:T(8,128)(2,1)S(1)}, u32[]{:S(2)}, u32[]{:S(2)}) collective-permute-start(bf16[128,2048]{1,0:T(8,128)(2,1)S(1)} %add_convert_fusion.3), channel_id=1, source_target_pairs={{0,16},{1,17},{2,18},{3,19},{4,20},{5,21},{6,22},{7,23},{8,24},{9,... | collective-permute-start | bytes 1572872 | tf_op jit(solution)/shard_map/ppermute | solution.py:339
  190.8 15.4 %collective-permute-start.31 = (bf16[128,2048]{1,0:T(8,128)(2,1)S(1)}, bf16[128,2048]{1,0:T(8,128)(2,1)S(1)}, u32[]{:S(2)}, u32[]{:S(2)}) collective-permute-start(bf16[128,2048]{1,0:T(8,128)(2,1)S(1)} %add_convert_fusion), channel_id=1, source_target_pairs={{0,8},{1,9},{2,10},{3,11},{4,12},{5,13},{6,14},{7,15},{8,16},{9,17... | collective-permute-start | bytes 1572872 | tf_op jit(solution)/shard_map/ppermute | solution.py:339
  (36 other events, 851.3 us)
Sparse Core Ops, SparseCore 0:
  208.1 21.3 all-gather.1
